TPU v7x, 32 devices: a whole 2x2x4 slice. The times are simulated.
32 devices in a mesh: mem: 8 (over y, x, core), tile: 4 (over z).
Axes of the slice: x: 2, y: 2, z: 4, core: 2. Of those that a mesh axis runs over, the one named last changes fastest.
Arguments:
- starting_ensemble: bfloat16 [16, 8, 32, 1120], P('mem', None, 'tile'), may hold values from -6 to 6
- patch_lifting: bfloat16 [1120, 768], P('mem'), may hold values from -0.1875 to 0.1875
- query_keyvalue_lift: bfloat16 [768, 2304], P(None, 'mem'), may hold values from -0.21875 to 0.21875
- output_combiner: bfloat16 [768, 768], P(None, 'mem'), may hold values from -0.21875 to 0.21875
- decoder_linear_map: bfloat16 [768, 1120], P(None, 'mem'), may hold values from -0.21875 to 0.21875
- cosine_logit_scale: float32 [12], replicated, may hold values from 2 to 30
- sensor_variable_loadings: bfloat16 [16, 70], replicated, may hold values from -0.75 to 0.75
- sensor_gridpoint: int32 [8, 4, 256], P('mem', 'tile'), may hold values from 0 to 127, as said below
- sensor_domain_index: int32 [8, 4, 256], P('mem', 'tile'), may hold values from 0 to 7, as said below
- sensor_channel_list: int32 [8, 4, 256], P('mem', 'tile'), may hold values from 0 to 15
- sensor_reading: float32 [8, 4, 256], P('mem', 'tile'), may hold values from -6 to 6
- sensor_noise_deviation: float32 [8, 4, 256], P('mem', 'tile'), may hold values from 0.5 to 2
Outputs:
- analysis: bfloat16 [16, 8, 32, 1120], P('mem', None, 'tile')
Inputs may be any that keep to these rules, and one draw needn't show every extreme that they name: `sensor_gridpoint`: a point of the piece's 8 tokens. `sensor_domain_index`: differs by at most one from sensor_gridpoint // 16 of the same observation.
All inputs are finite; a program needn't handle non-finite values. Where the computation divides by a largest or mean magnitude, that divisor is 1e-20 or more.
Results may differ from a plain program's by a relative error of at most 0.039.
Values may be sent and summed in bfloat16 or wider, within the bound.
A program may use at most 64 MiB of HBM per device.

v0:
```python
import jax
import jax.numpy as jnp
from jax import lax
from jax.sharding import PartitionSpec as P

PANE_SIDE = 8
NS_ITERS = 5


eps_norm = 1e-05
normalizing_guard = 1e-06


def passed_along(value, axis, by):
    devices = lax.axis_size(axis)
    return lax.ppermute(value, axis, [(i, (i + by) % devices) for i in range(devices)])


def layer_norm(values):
    values = values.astype(jnp.float32)
    center = values - jnp.mean(values, axis=-1, keepdims=True)
    spread = jnp.mean(center * center, axis=-1, keepdims=True)
    return center * lax.rsqrt(spread + eps_norm)


def unit_rows(values):
    values = values.astype(jnp.float32)
    return (
        values * lax.rsqrt(jnp.sum(values * values, axis=-1, keepdims=True) + normalizing_guard)
    ).astype(jnp.bfloat16)


def pane_cosine_mixer(padded_part, query_keyvalue_lift, cosine_logit_scale):
    members, rows, cols, attention_span = padded_part.shape
    focus_groups = cosine_logit_scale.shape[0]
    head_dim = attention_span // focus_groups
    qkv = jnp.dot(
        padded_part.reshape(-1, attention_span),
        query_keyvalue_lift,
        preferred_element_type=jnp.float32,
    ).astype(jnp.bfloat16)
    qkv = qkv.reshape(
        members, rows // PANE_SIDE, PANE_SIDE, cols // PANE_SIDE, PANE_SIDE, 3 * attention_span
    )
    qkv = qkv.transpose(0, 1, 3, 2, 4, 5).reshape(
        -1, PANE_SIDE * PANE_SIDE, 3, focus_groups, head_dim
    )
    query = unit_rows(qkv[:, :, 0])
    key_rows = unit_rows(qkv[:, :, 1])
    value_rows = qkv[:, :, 2]
    affinity_logits = jnp.einsum(
        "bihd,bjhd->bhij", query, key_rows, preferred_element_type=jnp.float32
    )
    affinity_logits = affinity_logits * cosine_logit_scale[None, :, None, None]
    weights = jnp.exp(affinity_logits)
    probs = (weights / jnp.sum(weights, axis=-1, keepdims=True)).astype(jnp.bfloat16)
    mixed_outcome = jnp.einsum(
        "bhij,bjhd->bihd", probs, value_rows, preferred_element_type=jnp.float32
    )
    mixed_outcome = mixed_outcome.astype(jnp.bfloat16).reshape(
        members, rows // PANE_SIDE, cols // PANE_SIDE, PANE_SIDE, PANE_SIDE, attention_span
    )
    return mixed_outcome.transpose(0, 1, 3, 2, 4, 5).reshape(members, rows, cols, attention_span)


def batched(left, right):
    return jnp.einsum("rij,rjk->rik", left, right, precision=lax.Precision.HIGHEST)


def local_analysis(
    embedded_patches,
    decoder_linear_map,
    sensor_gridpoint,
    sensor_domain_index,
    sensor_channel_list,
    sensor_reading,
    sensor_noise_deviation,
    sensor_variable_loadings,
):
    members, regions, attention_span = embedded_patches.shape
    feats = decoder_linear_map.shape[1]
    channels, variables = sensor_variable_loadings.shape
    points = feats // variables
    count = sensor_gridpoint.shape[0]
    prior_member_grids = jnp.dot(
        embedded_patches.reshape(-1, attention_span),
        decoder_linear_map,
        preferred_element_type=jnp.float32,
    ).astype(jnp.bfloat16)
    token = sensor_gridpoint // points
    point = sensor_gridpoint - token * points
    pick_point = (point[:, None] == jnp.arange(points, dtype=jnp.int32)[None, :]).astype(
        jnp.float32
    )
    pick_chan = (
        sensor_channel_list[:, None] == jnp.arange(channels, dtype=jnp.int32)[None, :]
    ).astype(jnp.float32)
    rows_h = jnp.dot(
        pick_chan, sensor_variable_loadings.astype(jnp.float32), precision=lax.Precision.HIGHEST
    )
    measurement_mapping = (
        (pick_point[:, :, None] * rows_h[:, None, :]).reshape(count, feats).astype(jnp.bfloat16)
    )
    mapped_samples = lax.dot_general(
        prior_member_grids,
        measurement_mapping,
        (((1,), (1,)), ((), ())),
        preferred_element_type=jnp.float32,
    )
    mapped_samples = mapped_samples.reshape(members, regions, count)
    pick_token = (token[None, :] == jnp.arange(regions, dtype=jnp.int32)[:, None]).astype(
        jnp.float32
    )
    ens_obs = jnp.sum(mapped_samples * pick_token[None], axis=1)
    mean_obs = jnp.mean(ens_obs, axis=0)
    pert_obs = ens_obs - mean_obs[None, :]
    innovation = sensor_reading - mean_obs
    distance = (token - sensor_domain_index).astype(jnp.float32)
    obs_weight = jnp.exp(-0.5 * distance * distance) / (
        sensor_noise_deviation * sensor_noise_deviation
    )
    pick_region = (
        sensor_domain_index[:, None] == jnp.arange(regions, dtype=jnp.int32)[None, :]
    ).astype(jnp.float32)
    weighted = pert_obs * obs_weight[None, :]
    gram = jnp.einsum(
        "kj,jr,lj->rkl", weighted, pick_region, pert_obs, precision=lax.Precision.HIGHEST
    )
    drive = jnp.einsum(
        "kj,jr,j->rk", weighted, pick_region, innovation, precision=lax.Precision.HIGHEST
    )
    eye = jnp.eye(members, dtype=jnp.float32)
    system = eye[None] + gram / (members - 1.0)
    bound = jnp.max(jnp.sum(jnp.abs(system), axis=2), axis=1)
    iterate = system / bound[:, None, None]
    inverse_root = jnp.broadcast_to(eye, system.shape)
    for step in range(NS_ITERS):
        factor = 1.5 * eye[None] - 0.5 * batched(inverse_root, iterate)
        iterate = batched(iterate, factor)
        inverse_root = batched(factor, inverse_root)
    root = inverse_root * lax.rsqrt(bound)[:, None, None]
    inner = jnp.einsum("rkl,rl->rk", root, drive, precision=lax.Precision.HIGHEST)
    mean_weight = jnp.einsum("rkl,rl->rk", root, inner, precision=lax.Precision.HIGHEST) / (
        members - 1.0
    )
    transform_matrix = root + mean_weight[:, :, None]
    values = embedded_patches.astype(jnp.float32)
    center = jnp.mean(values, axis=0)
    spread = values - center[None]
    posterior = center[None] + jnp.einsum(
        "ktf,tkm->mtf", spread, transform_matrix, precision=lax.Precision.HIGHEST
    )
    return posterior.astype(jnp.bfloat16)


def per_device(
    starting_ensemble,
    patch_lifting,
    query_keyvalue_lift,
    output_combiner,
    decoder_linear_map,
    cosine_logit_scale,
    sensor_variable_loadings,
    sensor_gridpoint,
    sensor_domain_index,
    sensor_channel_list,
    sensor_reading,
    sensor_noise_deviation,
):
    members, rows, cols, feats = starting_ensemble.shape
    full_embed, entire_triplet_product, full_out, full_head = (
        lax.all_gather(patch_lifting, "mem", axis=0, tiled=True),
        lax.all_gather(query_keyvalue_lift, "mem", axis=1, tiled=True),
        lax.all_gather(output_combiner, "mem", axis=1, tiled=True),
        lax.all_gather(decoder_linear_map, "mem", axis=1, tiled=True),
    )
    attention_span = full_embed.shape[1]
    hidden = jnp.dot(
        starting_ensemble.reshape(-1, feats), full_embed, preferred_element_type=jnp.float32
    )
    hidden = hidden.astype(jnp.bfloat16).reshape(members, rows, cols, attention_span)
    normed = layer_norm(hidden).astype(jnp.bfloat16)
    half = PANE_SIDE // 2
    incoming_rows = passed_along(normed[:, :, :half], "tile", -1)
    padded_sequence = jnp.concatenate([normed[:, :, half:], incoming_rows], axis=2)
    mixed_outcome_padded = pane_cosine_mixer(
        padded_sequence, entire_triplet_product, cosine_logit_scale
    )
    returned = passed_along(mixed_outcome_padded[:, :, cols - half :], "tile", 1)
    mixed_outcome = jnp.concatenate([returned, mixed_outcome_padded[:, :, : cols - half]], axis=2)
    mixed = hidden.astype(jnp.float32) + jnp.dot(
        mixed_outcome.reshape(-1, attention_span), full_out, preferred_element_type=jnp.float32
    ).reshape(members, rows, cols, attention_span)
    embedded_patches = layer_norm(mixed).astype(jnp.bfloat16)
    tile_tokens = rows * cols
    moved = lax.all_to_all(
        embedded_patches.reshape(members, tile_tokens, attention_span),
        "mem",
        split_axis=1,
        concat_axis=0,
        tiled=True,
    )
    ensemble, regions = (moved.shape[0], moved.shape[1])
    posterior = local_analysis(
        moved,
        full_head,
        sensor_gridpoint.reshape(-1),
        sensor_domain_index.reshape(-1),
        sensor_channel_list.reshape(-1),
        sensor_reading.reshape(-1),
        sensor_noise_deviation.reshape(-1),
        sensor_variable_loadings,
    )
    produced = jnp.dot(
        posterior.reshape(-1, attention_span), full_head, preferred_element_type=jnp.float32
    )
    produced = produced.astype(jnp.bfloat16).reshape(ensemble, regions, feats)
    analysed = lax.all_to_all(produced, "mem", split_axis=0, concat_axis=1, tiled=True)
    return analysed.reshape(members, rows, cols, feats)


def solution(mesh):
    return jax.shard_map(
        per_device,
        mesh=mesh,
        in_specs=(
            P("mem", None, "tile", None),
            P("mem", None),
            P(None, "mem"),
            P(None, "mem"),
            P(None, "mem"),
            P(),
            P(),
            P("mem", "tile", None),
            P("mem", "tile", None),
            P("mem", "tile", None),
            P("mem", "tile", None),
            P("mem", "tile", None),
        ),
        out_specs=P("mem", None, "tile", None),
        check_vma=False,
    )
```

profile of v0, /device:TPU:0, one launch (start us, length us, event | category | flops | bytes accessed | tf_op | source)
XLA Modules:
  0.0 156.3 jit_solution(16022520233245119169)
XLA Ops:
  6.5 0.7 all-gather.11.cloned.1.call-update
  7.3 0.7 all-gather.7.cloned.1.call-update
  8.1 0.7 all-gather.9.cloned.1.call-update
  8.8 0.5 all-gather.13.cloned.1.call-update
  9.3 0.8 mul.191
  10.1 0.7 fusion.57
  10.8 0.7 multiply_subtract_fusion
  11.5 0.9 fusion.29
  12.7 25.8 %all-gather.11.cloned.1.call-done = bf16[8,140,768]{2,1,0:T(8,128)(2,1)} async-done(((bf16[1,140,768]{2,1,0:T(8,128)(2,1)}), bf16[8,140,768]{2,1,0:T(8,128)(2,1)}) %all-gather.11.cloned.1.call-update) | async-done | bytes 1720336 | tf_op jit(solution)/shard_map/all_gather | solution.py:172
  38.5 1.6 %reshape.281 = bf16[1120,768]{1,0:T(8,128)(2,1)S(1)} reshape(bf16[8,140,768]{2,1,0:T(8,128)(2,1)} %all-gather.11.cloned.1.call-done) | data formatting | bytes 3440640
  40.1 0.5 fusion.71
  41.2 3.4 %collective-permute-start = (bf16[2,8,4,768]{3,2,1,0:T(4,128)(2,1)S(1)}, bf16[2,8,4,768]{3,2,1,0:T(4,128)(2,1)S(1)}, u32[]{:S(2)}, u32[]{:S(2)}) collective-permute-start(bf16[2,8,4,768]{3,2,1,0:T(4,128)(2,1)S(1)} %get-tuple-element.18), channel_id=1, source_target_pairs={{0,3},{1,0},{2,1},{3,2},{4,7},{5,4},{6,5},{7,6},{8,11},{9,8},{10,9... | collective-permute-start | bytes 294920 | tf_op jit(solution)/shard_map/ppermute | solution.py:16
  44.7 2.4 %collective-permute-done = bf16[2,8,4,768]{3,2,1,0:T(4,128)(2,1)S(1)} collective-permute-done((bf16[2,8,4,768]{3,2,1,0:T(4,128)(2,1)S(1)}, bf16[2,8,4,768]{3,2,1,0:T(4,128)(2,1)S(1)}, u32[]{:S(2)}, u32[]{:S(2)}) %collective-permute-start) | collective-permute-done | bytes 98336 | tf_op jit(solution)/shard_map/ppermute | solution.py:16
  47.2 27.2 %all-gather.7.cloned.1.call-done = bf16[768,2304]{0,1:T(8,128)(2,1)} async-done(((bf16[768,288]{0,1:T(8,128)(2,1)}), bf16[768,2304]{0,1:T(8,128)(2,1)}) %all-gather.7.cloned.1.call-update) | async-done | bytes 3538960 | tf_op jit(solution)/shard_map/all_gather | solution.py:173
  74.4 3.3 %convolution_convert_fusion = bf16[128,2304]{1,0:T(8,128)(2,1)S(1)} fusion(bf16[128,768]{1,0:T(8,128)(2,1)S(1)} %bitcast.130, bf16[768,2304]{0,1:T(8,128)(2,1)} %all-gather.7.cloned.1.call-done), kind=kOutput, calls=%fused_computation | convolution fusion | flops 453279744 | bytes 4325376 | tf_op jit(solution)/shard_map/dot_general | solution.py:37
  78.0 0.5 reshape_transpose_reshape.6
  78.8 1.0 fusion.12
  79.9 0.8 fusion.13
  82.1 1.5 collective-permute-start.1
  83.6 16.8 %all-gather.9.cloned.1.call-done = bf16[768,768]{0,1:T(8,128)(2,1)} async-done(((bf16[768,96]{0,1:T(8,128)(2,1)}), bf16[768,768]{0,1:T(8,128)(2,1)}) %all-gather.9.cloned.1.call-update) | async-done | bytes 1179664 | tf_op jit(solution)/shard_map/all_gather | solution.py:174
  100.4 1.9 %fusion.72 = (f32[2,8,8]{2,1,0:T(8,128)S(1)}, f32[2,8,8,768]{3,2,1,0:T(8,128)S(1)}) fusion(f32[2,8,8,768]{3,2,1,0:T(8,128)S(1)} %bitcast.127, bf16[768,768]{0,1:T(8,128)(2,1)} %all-gather.9.cloned.1.call-done, bf16[2,8,4,768]{3,2,1,0:T(4,128)(2,1)S(1)} %get-tuple-element.16, bf16[2,8,4,768]{3,2,1,0:T(4,128)(2,1)S(1)} %collective-permute-done.1), kind=kOutput, calls=%fused_computation.124 | convolution fusion | flops 151584640 | bytes 2163200 | tf_op jit(solution)/shard_map/dot_general | solution.py:191
  102.6 0.9 copy.107
  103.5 3.6 %all-to-all-start = ((bf16[2,64,768]{2,0,1:T(2,128)(2,1)}), bf16[2,64,768]{2,0,1:T(2,128)(2,1)S(1)}, u32[]{:S(2)}, u32[]{:S(2)}) async-start(bf16[2,64,768]{2,0,1:T(2,128)(2,1)} %copy.107), calls=%async_computation | async-start | bytes 393216 | tf_op jit(solution)/shard_map/all_to_all | solution.py:196
  107.1 21.6 %all-gather.13.cloned.1.call-done = bf16[8,140,768]{2,1,0:T(8,128)(2,1)} async-done(((bf16[1,140,768]{2,1,0:T(8,128)(2,1)}), bf16[8,140,768]{2,1,0:T(8,128)(2,1)}) %all-gather.13.cloned.1.call-update) | async-done | bytes 1720336 | tf_op jit(solution)/shard_map/all_gather | solution.py:175
  128.7 1.6 %reshape.283 = bf16[1120,768]{1,0:T(8,128)(2,1)S(1)} reshape(bf16[8,140,768]{2,1,0:T(8,128)(2,1)} %all-gather.13.cloned.1.call-done) | data formatting | bytes 3440640
  130.4 1.3 convolution_convert_fusion.2
  131.7 1.2 copy.111
  133.2 0.6 abs_reduce_fusion
  137.7 0.7 fusion.5
  138.4 0.6 convolution_convert_fusion.1
  139.2 9.8 %all_to_all.30 = bf16[16,8,1120]{2,1,0:T(8,128)(2,1)S(1)} all-to-all(bf16[16,8,1120]{2,1,0:T(8,128)(2,1)S(1)} %bitcast.128), channel_id=1, replica_groups=mesh['mem'=8,'tile'=4] {'mem'}, dimensions={0} | all-to-all | bytes 573440 | tf_op jit(solution)/shard_map/all_to_all | solution.py:218
  149.0 0.7 copy.121
  (72 shorter events, 7.8 us)
Async XLA Ops:
  6.5 33.6 %copy-start = (bf16[2,8,8,1120]{3,2,1,0:T(8,128)(2,1)S(1)}, bf16[2,8,8,1120]{3,2,1,0:T(8,128)(2,1)}, u32[]{:S(2)}) copy-start(bf16[2,8,8,1120]{3,2,1,0:T(8,128)(2,1)} %param.12) | copy-start | bytes 860164
  6.5 32.0 %all-gather.11.cloned.1.call-start = ((), (), s32[]{:S(2)}) async-start(), calls=%async_computation.4 | async-start | bytes 1990656 | tf_op jit(solution)/shard_map/all_gather | solution.py:172
  7.3 67.1 %all-gather.7.cloned.1.call-start = ((), (), s32[]{:S(2)}) async-start(), calls=%async_computation.2 | async-start | bytes 3981312 | tf_op jit(solution)/shard_map/all_gather | solution.py:173
  8.0 92.4 %all-gather.9.cloned.1.call-start = ((), (), s32[]{:S(2)}) async-start(), calls=%async_computation.3 | async-start | bytes 1327104 | tf_op jit(solution)/shard_map/all_gather | solution.py:174
  8.7 119.9 %all-gather.13.cloned.1.call-start = ((), (), s32[]{:S(2)}) async-start(), calls=%async_computation.5 | async-start | bytes 1990656 | tf_op jit(solution)/shard_map/all_gather | solution.py:175
  41.2 5.9 %collective-permute-start = (bf16[2,8,4,768]{3,2,1,0:T(4,128)(2,1)S(1)}, bf16[2,8,4,768]{3,2,1,0:T(4,128)(2,1)S(1)}, u32[]{:S(2)}, u32[]{:S(2)}) collective-permute-start(bf16[2,8,4,768]{3,2,1,0:T(4,128)(2,1)S(1)} %get-tuple-element.18), channel_id=1, source_target_pairs={{0,3},{1,0},{2,1},{3,2},{4,7},{5,4},{6,5},{7,6},{8,11},{9,8},{10,9... | collective-permute-start | bytes 294920 | tf_op jit(solution)/shard_map/ppermute | solution.py:16
  78.5 2.2 %copy-start.3 = (f32[12]{0:T(128)S(1)}, f32[12]{0:T(128)}, u32[]{:S(2)}) copy-start(f32[12]{0:T(128)} %param.17) | copy-start | bytes 148
  82.1 18.3 %collective-permute-start.1 = (bf16[2,8,4,768]{3,2,1,0:T(4,128)(2,1)S(1)}, bf16[2,8,4,768]{3,2,1,0:T(4,128)(2,1)S(1)}, u32[]{:S(2)}, u32[]{:S(2)}) collective-permute-start(bf16[2,8,4,768]{3,2,1,0:T(4,128)(2,1)S(1)} %get-tuple-element.15), channel_id=1, source_target_pairs={{0,1},{1,2},{2,3},{3,0},{4,5},{5,6},{6,7},{7,4},{8,9},{9,10},{10,1... | collective-permute-start | bytes 294920 | tf_op jit(solution)/shard_map/ppermute | solution.py:16
  100.4 6.7 %copy-start.1 = (s32[1,1,256]{2,1,0:T(1,128)S(1)}, s32[1,1,256]{2,1,0:T(1,128)}, u32[]{:S(2)}) copy-start(s32[1,1,256]{2,1,0:T(1,128)} %param.20) | copy-start | bytes 3076
  103.5 26.8 %all-to-all-start = ((bf16[2,64,768]{2,0,1:T(2,128)(2,1)}), bf16[2,64,768]{2,0,1:T(2,128)(2,1)S(1)}, u32[]{:S(2)}, u32[]{:S(2)}) async-start(bf16[2,64,768]{2,0,1:T(2,128)(2,1)} %copy.107), calls=%async_computation | async-start | bytes 393216 | tf_op jit(solution)/shard_map/all_to_all | solution.py:196
  130.4 2.8 %copy-start.2 = (f32[1,1,256]{2,1,0:T(1,128)S(1)}, f32[1,1,256]{2,1,0:T(1,128)}, u32[]{:S(2)}) copy-start(f32[1,1,256]{2,1,0:T(1,128)} %param.22) | copy-start | bytes 3076
Sparse Core Ops, SparseCore 0:
  9.2 29.2 all-gather.10
  40.4 33.9 all-gather.6
  76.3 24.0 all-gather.8
  102.1 26.5 all-gather.12
where the time goes:
time: 157 us; the launch traced here: 156 us
  waiting for transfers between devices  96.3 us (61%)
  matrix products  14.3 us (9%)
  between operations  13.6 us (9%)
  blocking collectives  9.82 us (6%)
  starting transfers between devices  8.61 us (5%)
  local copies, waits for them, and re-layouts  8.58 us (5%)
  other arithmetic  5.09 us (3%)
    all_gather x1, waiting for transfers between devices, per_device(): lax.all_gather(query_keyvalue_lift, 'mem', axis=1, tiled=True)  27.2 us
    all_gather x1, waiting for transfers between devices, per_device(): lax.all_gather(patch_lifting, 'mem', axis=0, tiled=True)  25.8 us
    all_gather x1, waiting for transfers between devices, per_device(): lax.all_gather(decoder_linear_map, 'mem', axis=1, tiled=True)  21.6 us
    all_gather x1, waiting for transfers between devices, per_device(): lax.all_gather(output_combiner, 'mem', axis=1, tiled=True)  16.8 us
    all_to_all x1, blocking collectives, per_device(): lax.all_to_all(produced, 'mem', split_axis=0, concat_axis=1, tiled=True)  9.82 us
    ppermute x2, starting transfers between devices, passed_along(): lax.ppermute(value, axis, [(i, (i + by) % devices) for i in range(devices)])  4.92 us
    all_to_all x1, starting transfers between devices, per_device(): lax.all_to_all(embedded_patches.reshape(members, tile_tokens, attention_s...  3.57 us
    dot_general x1, matrix products, pane_cosine_mixer(): jnp.dot(padded_part.reshape(-1, attention_span), query_keyvalue_lift, pre...  3.29 us
  transfers between devices with their start and end apart: 7, of which 5 were waited for; matrix products, arithmetic and copies ran while one was open for 12% of the time, Pallas kernels for 0%

commit v1 on v0

--- a/solution.py
+++ b/solution.py
@@ -1,10 +1,17 @@
+import functools
+
 import jax
 import jax.numpy as jnp
 from jax import lax
+from jax.experimental import pallas as pl
+from jax.experimental.pallas import tpu as pltpu
 from jax.sharding import PartitionSpec as P
 
 PANE_SIDE = 8
 NS_ITERS = 5
+KINDS = 15
+MESH = pl.DeviceIdType.MESH
+HIGHEST = lax.Precision.HIGHEST
 
 
 eps_norm = 1e-05
@@ -219,24 +226,493 @@
     return analysed.reshape(members, rows, cols, feats)
 
 
+def iota(shape, dim):
+    return lax.broadcasted_iota(jnp.int32, shape, dim)
+
+
+def dot(left, right):
+    return jnp.dot(left, right, preferred_element_type=jnp.float32)
+
+
+def dot_nt(left, right):
+    return lax.dot_general(
+        left, right, (((1,), (1,)), ((), ())), preferred_element_type=jnp.float32
+    )
+
+
+def exact(left, right):
+    return jnp.dot(left, right, precision=HIGHEST, preferred_element_type=jnp.float32)
+
+
+def one_hot(mask):
+    return jnp.where(mask, 1.0, 0.0).astype(jnp.bfloat16)
+
+
+def picked(rows, source):
+    return one_hot(source == iota((rows, rows), 1))
+
+
+def forecast_and_analyse(
+    heads,
+    x_ref,
+    embed_ref,
+    qkv_ref,
+    comb_ref,
+    dec_ref,
+    scale_ref,
+    load_ref,
+    grid_ref,
+    dom_ref,
+    chan_ref,
+    read_ref,
+    noise_ref,
+    out_ref,
+    g_embed,
+    g_qkv,
+    g_comb,
+    g_dec,
+    x_pad,
+    to_west,
+    window,
+    qkv_buf,
+    ctx,
+    from_west,
+    lat_send,
+    lat_recv,
+    pos_send,
+    pos_recv,
+    w_send,
+    w_recv,
+    t_send,
+    t_recv,
+    a_send,
+    a_recv,
+):
+    bf16, f32 = jnp.bfloat16, jnp.float32
+    me = lax.axis_index("mem")
+    tile = lax.axis_index("tile")
+    tiles = lax.axis_size("tile")
+    n = lax.axis_size("mem")
+    core = me % 2
+    along_x = (me // 2) % 2
+    along_y = me // 4
+    to_sib = 1 - 2 * core
+    sib = me + to_sib
+    x_nb = me + 2 - 4 * along_x
+    y_nb = me + 4 - 8 * along_y
+    diag = x_nb + 4 - 8 * along_y
+    odd = tile % 2
+    partner = tile + 1 - 2 * odd
+    west = (tile + tiles - 1) % tiles
+    east = (tile + 1) % tiles
+
+    tokens, span = window.shape
+    half = tokens // 2
+    feats = x_ref.shape[1]
+    piece = feats // n
+    padded = g_embed.shape[0] // n
+    width = padded * n
+    count = grid_ref.shape[2]
+    variables = load_ref.shape[1]
+
+    barrier = pltpu.get_barrier_semaphore()
+    for step in range(1, n):
+        pl.semaphore_signal(
+            barrier, inc=1, device_id=((me + step) % n, tile), device_id_type=MESH
+        )
+    for other in (west, east):
+        pl.semaphore_signal(barrier, inc=1, device_id=(me, other), device_id_type=MESH)
+
+    gathered = (g_embed, g_qkv, g_comb, g_dec)
+    sends = []
+
+    def copy(w, kind, owner, first, rows, target):
+        held = gathered[w]
+        block = held.shape[0] // n
+        part = held.at[pl.ds(pl.multiple_of(owner * block + first, 16), rows)]
+        return pltpu.make_async_remote_copy(
+            src_ref=part,
+            dst_ref=part,
+            send_sem=w_send.at[w * KINDS + kind],
+            recv_sem=w_recv.at[w * KINDS + kind],
+            device_id=target,
+            device_id_type=MESH,
+        )
+
+    here = {
+        "sib": (sib, tile),
+        "x": (x_nb, tile),
+        "y": (y_nb, tile),
+        "z": (me, partner),
+    }
+
+    def send(w, kind, owner, first, rows, way):
+        sent = copy(w, kind, owner, first, rows, here[way])
+        sent.start()
+        sends.append(sent)
+
+    def arrived(w, kind, owner, first, rows):
+        copy(w, kind, owner, first, rows, here["sib"]).wait_recv()
+
+    def third(w):
+        return gathered[w].shape[0] // n // 3
+
+    def own(w):
+        t = third(w)
+        send(w, 1, me, odd * t, 2 * t, "x")
+        send(w, 2, me, odd * t, 2 * t, "y")
+        send(w, 0, me, 0, 3 * t, "sib")
+
+    def pass_neighbours(w):
+        t = third(w)
+        arrived(w, 1, x_nb, odd * t, 2 * t)
+        send(w, 5, x_nb, 2 * odd * t, t, "y")
+        send(w, 9, x_nb, 2 * odd * t, t, "z")
+        send(w, 3, x_nb, odd * t, 2 * t, "sib")
+        arrived(w, 2, y_nb, odd * t, 2 * t)
+        send(w, 6, y_nb, t, t, "x")
+        send(w, 10, y_nb, 2 * odd * t, t, "z")
+        send(w, 4, y_nb, odd * t, 2 * t, "sib")
+
+    def pass_diagonal(w):
+        t = third(w)
+        arrived(w, 5, diag, 2 * odd * t, t)
+        send(w, 11, diag, 2 * odd * t, t, "z")
+        send(w, 7, diag, 2 * odd * t, t, "sib")
+        arrived(w, 6, diag, t, t)
+        send(w, 8, diag, t, t, "sib")
+
+    def pass_partner(w):
+        t = third(w)
+        for kind, owner in ((9, x_nb), (10, y_nb), (11, diag)):
+            arrived(w, kind, owner, 2 * (1 - odd) * t, t)
+            send(w, kind + 3, owner, 2 * (1 - odd) * t, t, "sib")
+
+    def complete(w):
+        t = third(w)
+        arrived(w, 0, sib, 0, 3 * t)
+        arrived(w, 3, x_nb + to_sib, odd * t, 2 * t)
+        arrived(w, 4, y_nb + to_sib, odd * t, 2 * t)
+        arrived(w, 7, diag + to_sib, 2 * odd * t, t)
+        arrived(w, 8, diag + to_sib, t, t)
+        for kind, owner in ((12, x_nb), (13, y_nb), (14, diag)):
+            arrived(w, kind, owner + to_sib, 2 * (1 - odd) * t, t)
+
+    def keep_own(w, value):
+        block = gathered[w].shape[0] // n
+        gathered[w][pl.ds(pl.multiple_of(me * block, 16), block), :] = value.astype(bf16)
+
+    def eye(rows, cols):
+        return one_hot(iota((rows, cols), 0) == iota((rows, cols), 1))
+
+    EMBED, QKV, COMB, DEC = 0, 1, 2, 3
+
+    keep_own(EMBED, dot(eye(padded, piece), embed_ref[...]))
+    pl.semaphore_wait(barrier, n + 1)
+    own(EMBED)
+    keep_own(QKV, dot_nt(eye(qkv_ref.shape[1], qkv_ref.shape[1]), qkv_ref[...]))
+    own(QKV)
+    keep_own(COMB, dot_nt(eye(comb_ref.shape[1], comb_ref.shape[1]), comb_ref[...]))
+    keep_own(DEC, dot_nt(eye(padded, piece), dec_ref[...]))
+
+    row = iota((tokens, tokens), 0)
+    by_half = picked(
+        tokens,
+        ((row >> 5) & 1) * 64 + ((row >> 2) & 7) * 8 + (row >> 6) * 4 + (row & 3),
+    )
+    x_rows = dot(by_half, x_ref[...]).astype(bf16)
+    x_pad[...] = jnp.zeros(x_pad.shape, bf16)
+    for d in range(n):
+        x_pad[:, padded * d : padded * d + piece] = x_rows[:, piece * d : piece * (d + 1)]
+
+    pass_neighbours(EMBED)
+    own(COMB)
+
+    within = iota((n, padded, variables), 1)
+    within = within - jnp.where(within >= variables, variables, 0)
+    pick_variable = one_hot(within == iota((n, padded, variables), 2)).reshape(width, variables)
+    channels = load_ref.shape[0]
+    loads = dot_nt(pick_variable, load_ref[...]).astype(bf16)
+    chan_hot = one_hot(jnp.broadcast_to(chan_ref[0], (channels, count)) == iota((channels, count), 0))
+    mapping = dot(loads, chan_hot)
+    grid_point = grid_ref[0]
+    points = feats // variables
+    token_row = grid_point >> 4
+    point_row = grid_point & (points - 1)
+    dom_row = dom_ref[0]
+    slot = iota((n, padded, count), 0) * 2 + jnp.where(
+        iota((n, padded, count), 1) >= variables, 1, 0
+    )
+    mapping = jnp.where(
+        slot.reshape(width, count) == jnp.broadcast_to(point_row, (width, count)), mapping, 0.0
+    ).astype(bf16)
+
+    pass_diagonal(EMBED)
+    pass_partner(EMBED)
+    complete(EMBED)
+
+    hidden = dot(x_pad[...], g_embed[...]).astype(bf16)
+    normed = layer_norm(hidden).astype(bf16)
+    to_west[...] = normed[:half]
+    window[half:, :] = normed[half:]
+
+    def along_tile(index, source, target, way):
+        return pltpu.make_async_remote_copy(
+            src_ref=source,
+            dst_ref=target,
+            send_sem=t_send.at[index],
+            recv_sem=t_recv.at[index],
+            device_id=(me, way),
+            device_id_type=MESH,
+        )
+
+    westward = along_tile(0, to_west, window.at[pl.ds(0, half)], west)
+    westward.start()
+    sends.append(westward)
+
+    pass_neighbours(QKV)
+    own(DEC)
+    pass_diagonal(QKV)
+    pass_neighbours(COMB)
+    pass_partner(QKV)
+    westward.wait_recv()
+    complete(QKV)
+
+    qkv_buf[...] = dot_nt(window[...], g_qkv[...]).astype(bf16)
+    pass_diagonal(COMB)
+    pass_neighbours(DEC)
+
+    side = span // heads
+    same_member = ((row >> 5) & 1) == ((iota((tokens, tokens), 1) >> 5) & 1)
+    for h in range(heads):
+        query = unit_rows(qkv_buf[:, side * h : side * (h + 1)])
+        key = unit_rows(qkv_buf[:, span + side * h : span + side * (h + 1)])
+        value = qkv_buf[:, 2 * span + side * h : 2 * span + side * (h + 1)]
+        weights = jnp.where(same_member, jnp.exp(dot_nt(query, key) * scale_ref[h]), 0.0)
+        probs = (weights / jnp.sum(weights, axis=-1, keepdims=True)).astype(bf16)
+        ctx[:, side * h : side * (h + 1)] = dot(probs, value).astype(bf16)
+        if h == heads // 2:
+            pass_partner(COMB)
+            pass_diagonal(DEC)
+
+    eastward = along_tile(1, ctx.at[pl.ds(0, half)], from_west, east)
+    eastward.start()
+    sends.append(eastward)
+    complete(COMB)
+    pass_partner(DEC)
+    own_half = dot_nt(ctx[half:, :], g_comb[...])
+    eastward.wait_recv()
+    mixed = hidden.astype(f32) + jnp.concatenate(
+        [dot_nt(from_west[...], g_comb[...]), own_half], axis=0
+    )
+    latent = layer_norm(mixed).astype(bf16)
+    by_region = picked(
+        tokens,
+        ((row >> 2) & 1) * 64 + ((row >> 3) & 1) * 32 + (row >> 4) * 4 + (row & 3),
+    )
+    lat_send[...] = dot(by_region, latent).astype(bf16)
+
+    block = tokens // n
+
+    def exchange(index, source, target):
+        mine = pl.ds(pl.multiple_of(me * block, 16), block)
+        for step in range(1, n):
+            to = (me + step) % n
+            sent = pltpu.make_async_remote_copy(
+                src_ref=source.at[pl.ds(pl.multiple_of(to * block, 16), block)],
+                dst_ref=target.at[mine],
+                send_sem=a_send.at[index * n + step],
+                recv_sem=a_recv.at[index * n + step],
+                device_id=(to, tile),
+                device_id_type=MESH,
+            )
+            sent.start()
+            sends.append(sent)
+        target[mine, :] = source[mine, :]
+
+    def exchanged(index, source, target):
+        for step in range(1, n):
+            origin = (me + n - step) % n
+            part = pl.ds(pl.multiple_of(origin * block, 16), block)
+            pltpu.make_async_remote_copy(
+                src_ref=source.at[part],
+                dst_ref=target.at[part],
+                send_sem=a_send.at[index * n + step],
+                recv_sem=a_recv.at[index * n + step],
+                device_id=(origin, tile),
+                device_id_type=MESH,
+            ).wait_recv()
+
+    exchange(0, lat_send, lat_recv)
+    complete(DEC)
+    exchanged(0, lat_send, lat_recv)
+
+    members, regions = tokens // n, n
+    members = tokens // regions
+    values = lat_recv[...]
+    prior = dot_nt(values, g_dec[...]).astype(bf16)
+    samples = dot(prior, mapping).reshape(members, regions, count)
+    region3 = iota((members, regions, count), 1)
+    samples = jnp.where(region3 == token_row[None], samples, 0.0)
+    ens_obs = jnp.sum(samples, axis=1, keepdims=True)
+    mean_obs = jnp.mean(ens_obs, axis=0, keepdims=True)
+    in_region = region3 == dom_row[None]
+    pert = jnp.where(in_region, ens_obs - mean_obs, 0.0).reshape(tokens, count)
+    innovation = read_ref[0] - mean_obs[0]
+    distance = (token_row - dom_row).astype(f32)
+    noise = noise_ref[0]
+    obs_weight = jnp.exp(-0.5 * distance * distance) / (noise * noise)
+    weighted = pert * obs_weight
+    gram = lax.dot_general(
+        weighted, pert, (((1,), (1,)), ((), ())), precision=HIGHEST, preferred_element_type=f32
+    )
+    drive = jnp.sum(weighted * innovation, axis=1, keepdims=True)
+    unit = jnp.where(row == iota((tokens, tokens), 1), 1.0, 0.0)
+    system = unit + gram * (1.0 / (members - 1.0))
+    sums = jnp.sum(jnp.abs(system), axis=1, keepdims=True).reshape(members, regions, 1)
+    bound = jnp.broadcast_to(
+        jnp.max(sums, axis=0, keepdims=True), (members, regions, 1)
+    ).reshape(tokens, 1)
+    iterate = system / bound
+    inverse_root = None
+    for step in range(NS_ITERS):
+        if step == 0:
+            factor = 1.5 * unit - 0.5 * iterate
+            inverse_root = factor
+        else:
+            factor = 1.5 * unit - 0.5 * exact(inverse_root, iterate)
+            inverse_root = exact(factor, inverse_root)
+        if step < NS_ITERS - 1:
+            iterate = exact(iterate, factor)
+    root = inverse_root * lax.rsqrt(bound)
+    inner = exact(root, jnp.broadcast_to(drive, (tokens, tokens)))
+    mean_weight = exact(root, inner) * (1.0 / (members - 1.0))
+    same_region = (row & (regions - 1)) == (iota((tokens, tokens), 1) & (regions - 1))
+    transform = jnp.where(same_region, root + mean_weight, 0.0)
+    latents = values.astype(f32).reshape(members, regions, span)
+    center = jnp.mean(latents, axis=0, keepdims=True)
+    spread = (latents - center).reshape(tokens, span)
+    posterior = jnp.broadcast_to(center, latents.shape).reshape(tokens, span) + exact(
+        transform.T, spread
+    )
+    pos_send[...] = posterior.astype(bf16)
+    exchange(1, pos_send, pos_recv)
+    exchanged(1, pos_send, pos_recv)
+    by_member = picked(tokens, ((row >> 3) & 7) * 16 + (row >> 6) * 8 + (row & 7))
+    analysed = dot_nt(dot(by_member, pos_recv[...]).astype(bf16), g_dec[...])
+    for d in range(n):
+        out_ref[:, piece * d : piece * (d + 1)] = analysed[
+            :, padded * d : padded * d + piece
+        ].astype(bf16)
+    for sent in sends:
+        sent.wait_send()
+
+
+def per_device_fused(
+    starting_ensemble,
+    patch_lifting,
+    query_keyvalue_lift,
+    output_combiner,
+    decoder_linear_map,
+    cosine_logit_scale,
+    sensor_variable_loadings,
+    *sensors,
+):
+    n = lax.axis_size("mem")
+    members, rows, cols, feats = starting_ensemble.shape
+    tokens = members * rows * cols
+    span = patch_lifting.shape[1]
+    padded = -(-patch_lifting.shape[0] // 48) * 48
+    vmem = pl.BlockSpec(memory_space=pltpu.VMEM)
+    smem = pl.BlockSpec(memory_space=pltpu.SMEM)
+
+    def held(*shape):
+        return pltpu.VMEM(shape, jnp.bfloat16)
+
+    out = pl.pallas_call(
+        functools.partial(forecast_and_analyse, cosine_logit_scale.shape[0]),
+        out_shape=jax.ShapeDtypeStruct((tokens, feats), jnp.bfloat16),
+        in_specs=[vmem] * 5 + [smem] + [vmem] * 6,
+        out_specs=vmem,
+        scratch_shapes=[
+            held(padded * n, span),
+            held(query_keyvalue_lift.shape[1] * n, span),
+            held(output_combiner.shape[1] * n, span),
+            held(padded * n, span),
+            held(tokens, padded * n),
+            held(tokens // 2, span),
+            held(tokens, span),
+            held(tokens, 3 * span),
+            held(tokens, span),
+            held(tokens // 2, span),
+            held(tokens, span),
+            held(tokens, span),
+            held(tokens, span),
+            held(tokens, span),
+            pltpu.SemaphoreType.DMA((4 * KINDS,)),
+            pltpu.SemaphoreType.DMA((4 * KINDS,)),
+            pltpu.SemaphoreType.DMA((2,)),
+            pltpu.SemaphoreType.DMA((2,)),
+            pltpu.SemaphoreType.DMA((2 * n,)),
+            pltpu.SemaphoreType.DMA((2 * n,)),
+        ],
+        compiler_params=pltpu.CompilerParams(
+            collective_id=0, has_side_effects=True, vmem_limit_bytes=48 * 1024 * 1024
+        ),
+        cost_estimate=pl.CostEstimate(
+            flops=2 * tokens * span * (3 * feats + 4 * span),
+            bytes_accessed=16 * 1024 * 1024,
+            transcendentals=0,
+        ),
+    )(
+        starting_ensemble.reshape(tokens, feats),
+        patch_lifting,
+        query_keyvalue_lift,
+        output_combiner,
+        decoder_linear_map,
+        cosine_logit_scale,
+        sensor_variable_loadings,
+        *sensors,
+    )
+    return out.reshape(members, rows, cols, feats)
+
+
+def fits_fused(mesh, starting_ensemble, patch_lifting, query_keyvalue_lift, output_combiner, loads):
+    n, tiles = mesh.shape["mem"], mesh.shape["tile"]
+    members, rows, cols, feats = starting_ensemble.shape
+    return (
+        n == 8
+        and tiles % 2 == 0
+        and tiles > 2
+        and (members // n, rows, cols // tiles) == (2, 8, 8)
+        and feats == 16 * loads.shape[1]
+        and query_keyvalue_lift.shape[1] % (48 * n) == 0
+        and output_combiner.shape[1] % (48 * n) == 0
+    )
+
+
 def solution(mesh):
-    return jax.shard_map(
-        per_device,
-        mesh=mesh,
-        in_specs=(
-            P("mem", None, "tile", None),
-            P("mem", None),
-            P(None, "mem"),
-            P(None, "mem"),
-            P(None, "mem"),
-            P(),
-            P(),
-            P("mem", "tile", None),
-            P("mem", "tile", None),
-            P("mem", "tile", None),
-            P("mem", "tile", None),
-            P("mem", "tile", None),
-        ),
-        out_specs=P("mem", None, "tile", None),
-        check_vma=False,
-    )
+    def whole(*args):
+        fused = fits_fused(mesh, args[0], args[1], args[2], args[3], args[6])
+        return jax.shard_map(
+            per_device_fused if fused else per_device,
+            mesh=mesh,
+            in_specs=(
+                P("mem", None, "tile", None),
+                P("mem", None),
+                P(None, "mem"),
+                P(None, "mem"),
+                P(None, "mem"),
+                P(),
+                P(),
+                P("mem", "tile", None),
+                P("mem", "tile", None),
+                P("mem", "tile", None),
+                P("mem", "tile", None),
+                P("mem", "tile", None),
+            ),
+            out_specs=P("mem", None, "tile", None),
+            check_vma=False,
+        )(*args)
+
+    return whole

time: 157 us -> 69.8 us (0.44)
  waiting for transfers between devices: 96.3 us -> 0 us
  Pallas kernels: 0 us -> 66.5 us
  matrix products: 14.3 us -> 0 us
  between operations: 13.6 us -> 0.14 us
  blocking collectives: 9.82 us -> 0 us
  starting transfers between devices: 8.61 us -> 0 us
  local copies, waits for them, and re-layouts: 8.58 us -> 3 us
  other arithmetic: 5.09 us -> 0 us
    all_gather x4 -> x0, waiting for transfers between devices: 91.3 us -> none  [the longest x1 27.2 us: per_device(): lax.all_gather(query_keyvalue_lift, 'mem', axis=1, tiled=True)]
    pallas_call x0 -> x1, Pallas kernels: none -> 66.5 us  [per_device_fused(): pl.pallas_call(functools.partial(forecast_and_analyse, cosine_logit_scale...]
    dot_general x28 -> x0, matrix products: 14.3 us -> none  [the longest x1 3.29 us: pane_cosine_mixer(): jnp.dot(padded_part.reshape(-1, attention_span), query_keyvalue_lift, pre...]
    all_to_all x1 -> x0, blocking collectives: 9.82 us -> none  [per_device(): lax.all_to_all(produced, 'mem', split_axis=0, concat_axis=1, tiled=True)]
    ppermute x2 -> x0, starting transfers between devices: 4.92 us -> none  [passed_along(): lax.ppermute(value, axis, [(i, (i + by) % devices) for i in range(devices)])]
    all_to_all x1 -> x0, starting transfers between devices: 3.57 us -> none  [per_device(): lax.all_to_all(embedded_patches.reshape(members, tile_tokens, attention_s...]
    unnamed x4 -> x0, waiting for transfers between devices: 2.61 us -> none
    ppermute x2 -> x0, waiting for transfers between devices: 2.41 us -> none  [passed_along(): lax.ppermute(value, axis, [(i, (i + by) % devices) for i in range(devices)])]
  transfers between devices with their start and end apart: 7 -> 0, of which waited for: 5 -> 0; matrix products, arithmetic and copies ran while one was open for 12% -> 0% of each run, Pallas kernels for 0% -> 0%
where the time goes in v1:
time: 69.8 us; the launch traced here: 69.6 us
  Pallas kernels  66.5 us (95%)
  local copies, waits for them, and re-layouts  3 us (4%)
    pallas_call x1, Pallas kernels, per_device_fused(): pl.pallas_call(functools.partial(forecast_and_analyse, cosine_logit_scale...  66.5 us
    unnamed x26, local copies, waits for them, and re-layouts  3 us

profile of v1, /device:TPU:0, one launch (start us, length us, event | category | flops | bytes accessed | tf_op | source)
XLA Modules:
  0.0 69.6 jit_solution(5668813445652460715)
XLA Ops:
  0.0 0.0 copy-start.10
  0.0 0.0 copy-start.9
  0.0 1.1 %copy.14.comb_ref = bf16[768,96]{1,0:T(8,128)(2,1)S(1)} copy(bf16[768,96]{0,1:T(8,128)(2,1)} %param.15) | data formatting | bytes 294912 | tf_op args[3]
  1.1 0.0 copy-done.10
  1.2 0.2 copy.15.dec_ref
  1.3 0.0 copy-done.9
  1.3 0.0 copy-start
  1.4 0.0 copy-start.1
  1.4 0.0 copy-start.2
  1.4 0.0 copy-start.3
  1.4 0.0 copy-start.4
  1.4 0.0 copy-start.5
  1.4 0.0 copy-start.6
  1.4 0.0 copy-start.7
  1.4 0.0 copy-start.8
  1.4 0.3 copy.13.qkv_ref
  1.8 0.5 copy-done
  2.3 0.1 copy-done.1
  2.4 0.0 copy-done.2
  2.4 0.0 copy-done.3
  2.4 0.0 copy-done.4
  2.4 0.0 copy-done.5
  2.4 0.0 copy-done.6
  2.4 0.0 copy-done.7
  2.4 0.0 copy-done.8
  2.4 66.5 %shard_map.118 = bf16[128,1120]{1,0:T(8,128)(2,1)S(1)} custom-call(bf16[128,1120]{1,0:T(8,128)(2,1)S(1)} %bitcast.3, bf16[140,768]{1,0:T(8,128)(2,1)S(1)} %copy-done.1, bf16[768,288]{1,0:T(8,128)(2,1)S(1)} %copy.13.qkv_ref, bf16[768,96]{1,0:T(8,128)(2,1)S(1)} %copy.14.comb_ref, bf16[768,140]{1,0:T(8,128)(2,1)S(1)} %copy.15.dec_ref, f32[12]{0:T(128)S(1)} %copy-done.8, ...), custom_call_target="tpu_custom_call" | custom-call | flops 1264582656 | bytes 16777216 | tf_op jit(solution)/shard_map/pallas_call | solution.py:632
  68.9 0.7 %copy.17 = bf16[2,8,8,1120]{3,2,1,0:T(8,128)(2,1)} copy(bf16[2,8,8,1120]{3,2,1,0:T(8,128)(2,1)S(1)} %bitcast.2) | data formatting | bytes 573440
Async XLA Ops:
  0.0 1.1 %copy-start.10 = (bf16[768,140]{0,1:T(8,128)(2,1)S(1)}, bf16[768,140]{0,1:T(8,128)(2,1)}, u32[]{:S(2)}) copy-start(bf16[768,140]{0,1:T(8,128)(2,1)} %param.16) | copy-start | bytes 645124
  0.0 1.3 %copy-start.9 = (bf16[768,288]{0,1:T(8,128)(2,1)S(1)}, bf16[768,288]{0,1:T(8,128)(2,1)}, u32[]{:S(2)}) copy-start(bf16[768,288]{0,1:T(8,128)(2,1)} %param.14) | copy-start | bytes 1327108
  1.3 1.0 %copy-start = (bf16[2,8,8,1120]{3,2,1,0:T(8,128)(2,1)S(1)}, bf16[2,8,8,1120]{3,2,1,0:T(8,128)(2,1)}, u32[]{:S(2)}) copy-start(bf16[2,8,8,1120]{3,2,1,0:T(8,128)(2,1)} %param.12) | copy-start | bytes 860164
  1.4 1.0 %copy-start.1 = (bf16[140,768]{1,0:T(8,128)(2,1)S(1)}, bf16[140,768]{1,0:T(8,128)(2,1)}, u32[]{:S(2)}) copy-start(bf16[140,768]{1,0:T(8,128)(2,1)} %embed_ref.1) | copy-start | bytes 645124
  1.4 1.0 %copy-start.2 = (bf16[16,70]{1,0:T(8,128)(2,1)S(1)}, bf16[16,70]{1,0:T(8,128)(2,1)}, u32[]{:S(2)}) copy-start(bf16[16,70]{1,0:T(8,128)(2,1)} %load_ref.1) | copy-start | bytes 6724
  1.4 1.0 %copy-start.3 = (s32[1,1,256]{2,1,0:T(1,128)S(1)}, s32[1,1,256]{2,1,0:T(1,128)}, u32[]{:S(2)}) copy-start(s32[1,1,256]{2,1,0:T(1,128)} %grid_ref.1) | copy-start | bytes 3076
  1.4 1.0 %copy-start.4 = (s32[1,1,256]{2,1,0:T(1,128)S(1)}, s32[1,1,256]{2,1,0:T(1,128)}, u32[]{:S(2)}) copy-start(s32[1,1,256]{2,1,0:T(1,128)} %dom_ref.1) | copy-start | bytes 3076
  1.4 1.0 %copy-start.5 = (s32[1,1,256]{2,1,0:T(1,128)S(1)}, s32[1,1,256]{2,1,0:T(1,128)}, u32[]{:S(2)}) copy-start(s32[1,1,256]{2,1,0:T(1,128)} %chan_ref.1) | copy-start | bytes 3076
  1.4 1.0 %copy-start.6 = (f32[1,1,256]{2,1,0:T(1,128)S(1)}, f32[1,1,256]{2,1,0:T(1,128)}, u32[]{:S(2)}) copy-start(f32[1,1,256]{2,1,0:T(1,128)} %read_ref.1) | copy-start | bytes 3076
  1.4 1.0 %copy-start.7 = (f32[1,1,256]{2,1,0:T(1,128)S(1)}, f32[1,1,256]{2,1,0:T(1,128)}, u32[]{:S(2)}) copy-start(f32[1,1,256]{2,1,0:T(1,128)} %noise_ref.1) | copy-start | bytes 3076
  1.4 1.0 %copy-start.8 = (f32[12]{0:T(128)S(1)}, f32[12]{0:T(128)}, u32[]{:S(2)}) copy-start(f32[12]{0:T(128)} %scale_ref.1) | copy-start | bytes 148

commit v2 on v1

--- a/solution.py
+++ b/solution.py
@@ -9,9 +9,8 @@
 
 PANE_SIDE = 8
 NS_ITERS = 5
-KINDS = 15
+KINDS = 17
 MESH = pl.DeviceIdType.MESH
-HIGHEST = lax.Precision.HIGHEST
 
 
 eps_norm = 1e-05
@@ -240,8 +239,26 @@
     )
 
 
-def exact(left, right):
-    return jnp.dot(left, right, precision=HIGHEST, preferred_element_type=jnp.float32)
+def two_terms(values):
+    high = values.astype(jnp.bfloat16)
+    return high, (values - high.astype(jnp.float32)).astype(jnp.bfloat16)
+
+
+def fine(left, right):
+    left_high, left_low = two_terms(left)
+    right_high, right_low = two_terms(right)
+    return dot(
+        jnp.concatenate([left_high, left_low], axis=1),
+        jnp.concatenate([right_high, right_high], axis=0),
+    ) + dot(left_high, right_low)
+
+
+def fine_nt(left, right):
+    left_high, left_low = two_terms(left)
+    right_high, right_low = two_terms(right)
+    return (
+        dot_nt(left_high, right_high) + dot_nt(left_low, right_high) + dot_nt(left_high, right_low)
+    )
 
 
 def one_hot(mask):
@@ -357,22 +374,32 @@
     def third(w):
         return gathered[w].shape[0] // n // 3
 
-    def own(w):
+    def own_first(w):
         t = third(w)
-        send(w, 1, me, odd * t, 2 * t, "x")
-        send(w, 2, me, odd * t, 2 * t, "y")
+        send(w, 1, me, 2 * odd * t, t, "x")
+        send(w, 2, me, 2 * odd * t, t, "y")
+
+    def own_second(w):
+        t = third(w)
+        send(w, 15, me, t, t, "x")
+        send(w, 16, me, t, t, "y")
         send(w, 0, me, 0, 3 * t, "sib")
 
-    def pass_neighbours(w):
+    def pass_first(w):
         t = third(w)
-        arrived(w, 1, x_nb, odd * t, 2 * t)
+        arrived(w, 1, x_nb, 2 * odd * t, t)
         send(w, 5, x_nb, 2 * odd * t, t, "y")
         send(w, 9, x_nb, 2 * odd * t, t, "z")
+        arrived(w, 2, y_nb, 2 * odd * t, t)
+        send(w, 10, y_nb, 2 * odd * t, t, "z")
+
+    def pass_second(w):
+        t = third(w)
+        arrived(w, 16, y_nb, t, t)
+        send(w, 6, y_nb, t, t, "x")
+        send(w, 4, y_nb, odd * t, 2 * t, "sib")
+        arrived(w, 15, x_nb, t, t)
         send(w, 3, x_nb, odd * t, 2 * t, "sib")
-        arrived(w, 2, y_nb, odd * t, 2 * t)
-        send(w, 6, y_nb, t, t, "x")
-        send(w, 10, y_nb, 2 * odd * t, t, "z")
-        send(w, 4, y_nb, odd * t, 2 * t, "sib")
 
     def pass_diagonal(w):
         t = third(w)
@@ -398,22 +425,27 @@
         for kind, owner in ((12, x_nb), (13, y_nb), (14, diag)):
             arrived(w, kind, owner + to_sib, 2 * (1 - odd) * t, t)
 
-    def keep_own(w, value):
+    def keep_own(w, ref):
         block = gathered[w].shape[0] // n
-        gathered[w][pl.ds(pl.multiple_of(me * block, 16), block), :] = value.astype(bf16)
-
-    def eye(rows, cols):
-        return one_hot(iota((rows, cols), 0) == iota((rows, cols), 1))
+        rows = ref.shape[0] // 16 * 16
+        gathered[w][pl.ds(pl.multiple_of(me * block, 16), rows), :] = ref[:rows, :]
+        if rows < block:
+            left = ref.shape[0] - rows
+            mask = one_hot(iota((block - rows, left), 0) == iota((block - rows, left), 1))
+            gathered[w][pl.ds(pl.multiple_of(me * block + rows, 16), block - rows), :] = dot(
+                mask, ref[rows:, :]
+            ).astype(bf16)
 
     EMBED, QKV, COMB, DEC = 0, 1, 2, 3
 
-    keep_own(EMBED, dot(eye(padded, piece), embed_ref[...]))
+    keep_own(EMBED, embed_ref)
+    keep_own(QKV, qkv_ref)
     pl.semaphore_wait(barrier, n + 1)
-    own(EMBED)
-    keep_own(QKV, dot_nt(eye(qkv_ref.shape[1], qkv_ref.shape[1]), qkv_ref[...]))
-    own(QKV)
-    keep_own(COMB, dot_nt(eye(comb_ref.shape[1], comb_ref.shape[1]), comb_ref[...]))
-    keep_own(DEC, dot_nt(eye(padded, piece), dec_ref[...]))
+    own_first(EMBED)
+    own_second(EMBED)
+    own_first(QKV)
+    keep_own(COMB, comb_ref)
+    keep_own(DEC, dec_ref)
 
     row = iota((tokens, tokens), 0)
     by_half = picked(
@@ -425,8 +457,9 @@
     for d in range(n):
         x_pad[:, padded * d : padded * d + piece] = x_rows[:, piece * d : piece * (d + 1)]
 
-    pass_neighbours(EMBED)
-    own(COMB)
+    pass_first(EMBED)
+    pass_second(EMBED)
+    own_second(QKV)
 
     within = iota((n, padded, variables), 1)
     within = within - jnp.where(within >= variables, variables, 0)
@@ -448,7 +481,10 @@
     ).astype(bf16)
 
     pass_diagonal(EMBED)
+    own_first(COMB)
+    pass_first(QKV)
     pass_partner(EMBED)
+    own_second(COMB)
     complete(EMBED)
 
     hidden = dot(x_pad[...], g_embed[...]).astype(bf16)
@@ -470,34 +506,61 @@
     westward.start()
     sends.append(westward)
 
-    pass_neighbours(QKV)
-    own(DEC)
+    pass_second(QKV)
+    own_first(DEC)
+    pass_first(COMB)
     pass_diagonal(QKV)
-    pass_neighbours(COMB)
+    own_second(DEC)
+    pass_second(COMB)
     pass_partner(QKV)
+    complete(QKV)
+    qkv_buf[half:, :] = dot_nt(window[half:, :], g_qkv[...]).astype(bf16)
+    pass_first(DEC)
+    pass_diagonal(COMB)
     westward.wait_recv()
-    complete(QKV)
-
-    qkv_buf[...] = dot_nt(window[...], g_qkv[...]).astype(bf16)
-    pass_diagonal(COMB)
-    pass_neighbours(DEC)
+    qkv_buf[:half, :] = dot_nt(window[:half, :], g_qkv[...]).astype(bf16)
+    pass_second(DEC)
 
     side = span // heads
-    same_member = ((row >> 5) & 1) == ((iota((tokens, tokens), 1) >> 5) & 1)
-    for h in range(heads):
-        query = unit_rows(qkv_buf[:, side * h : side * (h + 1)])
-        key = unit_rows(qkv_buf[:, span + side * h : span + side * (h + 1)])
-        value = qkv_buf[:, 2 * span + side * h : 2 * span + side * (h + 1)]
-        weights = jnp.where(same_member, jnp.exp(dot_nt(query, key) * scale_ref[h]), 0.0)
-        probs = (weights / jnp.sum(weights, axis=-1, keepdims=True)).astype(bf16)
-        ctx[:, side * h : side * (h + 1)] = dot(probs, value).astype(bf16)
-        if h == heads // 2:
-            pass_partner(COMB)
-            pass_diagonal(DEC)
-
+    pair = 2 * side
+    one_head = iota((pair, pair), 0) // side == iota((pair, pair), 1) // side
+    head_sum = one_hot(one_head)
+    head_sums = jnp.concatenate([head_sum, head_sum], axis=0)
+    lane = iota((tokens, pair), 1)
+    first = jnp.where(lane < side, 1.0, 0.0).astype(bf16)
+    second = jnp.where(lane < side, 0.0, 1.0).astype(bf16)
+    share = jnp.concatenate([first, second], axis=0)
+    key_of = iota((half, 2 * tokens), 1)
+    same_member = ((iota((half, 2 * tokens), 0) >> 5) & 1) == ((key_of >> 5) & 1)
+
+    def unit_pair(rows, start):
+        values = qkv_buf[rows, start : start + pair].astype(f32)
+        squares = jnp.concatenate(two_terms(values * values), axis=1)
+        return (values * lax.rsqrt(dot(squares, head_sums) + normalizing_guard)).astype(bf16)
+
+    def attend(rows, pairs):
+        for p in pairs:
+            start = pair * p
+            query = unit_pair(rows, start)
+            key = keys[p]
+            scales = jnp.where(key_of < tokens, scale_ref[2 * p], scale_ref[2 * p + 1])
+            weights = jnp.where(same_member, jnp.exp(dot_nt(query, key) * scales), 0.0).astype(bf16)
+            value = qkv_buf[:, 2 * span + start : 2 * span + start + pair]
+            value = jnp.concatenate([value * first, value * second], axis=0)
+            total = dot(weights, jnp.concatenate([value, share], axis=1))
+            ctx[rows, start : start + pair] = (total[:, :pair] / total[:, pair:]).astype(bf16)
+
+    keys = []
+    for p in range(heads // 2):
+        key = unit_pair(slice(None), span + pair * p)
+        keys.append(jnp.concatenate([key * first, key * second], axis=0))
+    attend(slice(0, half), range(heads // 2))
     eastward = along_tile(1, ctx.at[pl.ds(0, half)], from_west, east)
     eastward.start()
     sends.append(eastward)
+    pass_partner(COMB)
+    pass_diagonal(DEC)
+    attend(slice(half, tokens), range(heads // 2))
     complete(COMB)
     pass_partner(DEC)
     own_half = dot_nt(ctx[half:, :], g_comb[...])
@@ -547,7 +610,7 @@
     complete(DEC)
     exchanged(0, lat_send, lat_recv)
 
-    members, regions = tokens // n, n
+    regions = n
     members = tokens // regions
     values = lat_recv[...]
     prior = dot_nt(values, g_dec[...]).astype(bf16)
@@ -563,10 +626,8 @@
     noise = noise_ref[0]
     obs_weight = jnp.exp(-0.5 * distance * distance) / (noise * noise)
     weighted = pert * obs_weight
-    gram = lax.dot_general(
-        weighted, pert, (((1,), (1,)), ((), ())), precision=HIGHEST, preferred_element_type=f32
-    )
-    drive = jnp.sum(weighted * innovation, axis=1, keepdims=True)
+    gram = fine_nt(weighted, pert)
+    drive = fine_nt(jnp.broadcast_to(innovation, (tokens, count)), weighted)
     unit = jnp.where(row == iota((tokens, tokens), 1), 1.0, 0.0)
     system = unit + gram * (1.0 / (members - 1.0))
     sums = jnp.sum(jnp.abs(system), axis=1, keepdims=True).reshape(members, regions, 1)
@@ -580,20 +641,20 @@
             factor = 1.5 * unit - 0.5 * iterate
             inverse_root = factor
         else:
-            factor = 1.5 * unit - 0.5 * exact(inverse_root, iterate)
-            inverse_root = exact(factor, inverse_root)
+            factor = 1.5 * unit - 0.5 * fine(inverse_root, iterate)
+            inverse_root = fine(factor, inverse_root)
         if step < NS_ITERS - 1:
-            iterate = exact(iterate, factor)
+            iterate = fine(iterate, factor)
     root = inverse_root * lax.rsqrt(bound)
-    inner = exact(root, jnp.broadcast_to(drive, (tokens, tokens)))
-    mean_weight = exact(root, inner) * (1.0 / (members - 1.0))
+    inner = fine(drive, root)
+    mean_weight = fine(inner, root) * (1.0 / (members - 1.0))
     same_region = (row & (regions - 1)) == (iota((tokens, tokens), 1) & (regions - 1))
-    transform = jnp.where(same_region, root + mean_weight, 0.0)
+    transform_back = jnp.where(same_region, root + mean_weight, 0.0)
     latents = values.astype(f32).reshape(members, regions, span)
     center = jnp.mean(latents, axis=0, keepdims=True)
     spread = (latents - center).reshape(tokens, span)
-    posterior = jnp.broadcast_to(center, latents.shape).reshape(tokens, span) + exact(
-        transform.T, spread
+    posterior = jnp.broadcast_to(center, latents.shape).reshape(tokens, span) + fine(
+        transform_back, spread
     )
     pos_send[...] = posterior.astype(bf16)
     exchange(1, pos_send, pos_recv)
@@ -667,9 +728,9 @@
     )(
         starting_ensemble.reshape(tokens, feats),
         patch_lifting,
-        query_keyvalue_lift,
-        output_combiner,
-        decoder_linear_map,
+        query_keyvalue_lift.T,
+        output_combiner.T,
+        decoder_linear_map.T,
         cosine_logit_scale,
         sensor_variable_loadings,
         *sensors,

time: 69.8 us -> 68.9 us (0.987)
  Pallas kernels: 66.5 us -> 61 us
  local copies, waits for them, and re-layouts: 3 us -> 7.55 us
    pallas_call x1, Pallas kernels: 66.5 us -> 61 us  [per_device_fused(): pl.pallas_call(functools.partial(forecast_and_analyse, cosine_logit_scale...]
    unnamed x26 -> x25, local copies, waits for them, and re-layouts: 3 us -> 7.55 us
where the time goes in v2:
time: 68.9 us; the launch traced here: 68.6 us
  Pallas kernels  61 us (89%)
  local copies, waits for them, and re-layouts  7.55 us (11%)
    pallas_call x1, Pallas kernels, per_device_fused(): pl.pallas_call(functools.partial(forecast_and_analyse, cosine_logit_scale...  61 us
    unnamed x25, local copies, waits for them, and re-layouts  7.55 us

profile of v2, /device:TPU:0, one launch (start us, length us, event | category | flops | bytes accessed | tf_op | source)
XLA Modules:
  0.0 68.6 jit_solution(1174724051931615065)
XLA Ops:
  0.0 0.0 copy-start.5
  0.0 0.0 copy-start.7
  0.0 0.0 copy-start.8
  0.0 0.0 copy-start.6
  0.0 0.0 copy-start.11
  0.0 0.7 copy-done.5
  0.7 0.0 copy-done.7
  0.7 0.0 copy-done.8
  0.7 0.0 copy-done.6
  0.7 0.0 copy-done.11
  0.7 0.0 copy-start
  0.7 1.0 %copy-done = bf16[768,288]{0,1:T(8,128)(2,1)S(1)} copy-done((bf16[768,288]{0,1:T(8,128)(2,1)S(1)}, bf16[768,288]{0,1:T(8,128)(2,1)}, u32[]{:S(2)}) %copy-start) | copy-done | bytes 442392
  1.7 0.0 copy-start.1
  1.7 1.0 %copy-done.1 = bf16[2,8,8,1120]{3,2,1,0:T(8,128)(2,1)S(1)} copy-done((bf16[2,8,8,1120]{3,2,1,0:T(8,128)(2,1)S(1)}, bf16[2,8,8,1120]{3,2,1,0:T(8,128)(2,1)}, u32[]{:S(2)}) %copy-start.1) | copy-done | bytes 286744
  2.7 0.0 copy-start.2
  2.7 0.9 %copy-done.2 = bf16[140,768]{1,0:T(8,128)(2,1)S(1)} copy-done((bf16[140,768]{1,0:T(8,128)(2,1)S(1)}, bf16[140,768]{1,0:T(8,128)(2,1)}, u32[]{:S(2)}) %copy-start.2) | copy-done | bytes 215064
  3.6 0.0 copy-start.3
  3.6 0.9 %copy-done.3 = bf16[768,140]{0,1:T(8,128)(2,1)S(1)} copy-done((bf16[768,140]{0,1:T(8,128)(2,1)S(1)}, bf16[768,140]{0,1:T(8,128)(2,1)}, u32[]{:S(2)}) %copy-start.3) | copy-done | bytes 215064
  4.6 0.0 copy-start.4
  4.6 0.9 %copy-done.4 = bf16[768,96]{0,1:T(8,128)(2,1)S(1)} copy-done((bf16[768,96]{0,1:T(8,128)(2,1)S(1)}, bf16[768,96]{0,1:T(8,128)(2,1)}, u32[]{:S(2)}) %copy-start.4) | copy-done | bytes 147480
  5.5 0.0 copy-start.9
  5.5 0.7 copy-done.9
  6.2 0.0 copy-start.10
  6.2 0.7 copy-done.10
  6.8 61.0 %shard_map.118 = bf16[128,1120]{1,0:T(8,128)(2,1)S(1)} custom-call(bf16[128,1120]{1,0:T(8,128)(2,1)S(1)} %bitcast.7, bf16[140,768]{1,0:T(8,128)(2,1)S(1)} %copy-done.2, bf16[288,768]{1,0:T(8,128)(2,1)S(1)} %bitcast.6, bf16[96,768]{1,0:T(8,128)(2,1)S(1)} %bitcast.9, bf16[140,768]{1,0:T(8,128)(2,1)S(1)} %bitcast.8, f32[12]{0:T(128)S(1)} %copy-done.11, ...), custom_call_target="tpu_custom_call" | custom-call | flops 1264582656 | bytes 16777216 | tf_op jit(solution)/shard_map/pallas_call | solution.py:693
  67.9 0.7 %copy.14 = bf16[2,8,8,1120]{3,2,1,0:T(8,128)(2,1)} copy(bf16[2,8,8,1120]{3,2,1,0:T(8,128)(2,1)S(1)} %bitcast.5) | data formatting | bytes 573440
Async XLA Ops:
  0.0 0.7 %copy-start.5 = (bf16[16,70]{1,0:T(8,128)(2,1)S(1)}, bf16[16,70]{1,0:T(8,128)(2,1)}, u32[]{:S(2)}) copy-start(bf16[16,70]{1,0:T(8,128)(2,1)} %load_ref.1) | copy-start | bytes 6724
  0.0 0.7 %copy-start.7 = (s32[1,1,256]{2,1,0:T(1,128)S(1)}, s32[1,1,256]{2,1,0:T(1,128)}, u32[]{:S(2)}) copy-start(s32[1,1,256]{2,1,0:T(1,128)} %dom_ref.1) | copy-start | bytes 3076
  0.0 0.7 %copy-start.8 = (s32[1,1,256]{2,1,0:T(1,128)S(1)}, s32[1,1,256]{2,1,0:T(1,128)}, u32[]{:S(2)}) copy-start(s32[1,1,256]{2,1,0:T(1,128)} %chan_ref.1) | copy-start | bytes 3076
  0.0 0.7 %copy-start.6 = (s32[1,1,256]{2,1,0:T(1,128)S(1)}, s32[1,1,256]{2,1,0:T(1,128)}, u32[]{:S(2)}) copy-start(s32[1,1,256]{2,1,0:T(1,128)} %grid_ref.1) | copy-start | bytes 3076
  0.0 0.7 %copy-start.11 = (f32[12]{0:T(128)S(1)}, f32[12]{0:T(128)}, u32[]{:S(2)}) copy-start(f32[12]{0:T(128)} %scale_ref.1) | copy-start | bytes 148
  0.7 1.0 %copy-start = (bf16[768,288]{0,1:T(8,128)(2,1)S(1)}, bf16[768,288]{0,1:T(8,128)(2,1)}, u32[]{:S(2)}) copy-start(bf16[768,288]{0,1:T(8,128)(2,1)} %param.14) | copy-start | bytes 1327108
  1.7 1.0 %copy-start.1 = (bf16[2,8,8,1120]{3,2,1,0:T(8,128)(2,1)S(1)}, bf16[2,8,8,1120]{3,2,1,0:T(8,128)(2,1)}, u32[]{:S(2)}) copy-start(bf16[2,8,8,1120]{3,2,1,0:T(8,128)(2,1)} %param.12) | copy-start | bytes 860164
  2.7 0.9 %copy-start.2 = (bf16[140,768]{1,0:T(8,128)(2,1)S(1)}, bf16[140,768]{1,0:T(8,128)(2,1)}, u32[]{:S(2)}) copy-start(bf16[140,768]{1,0:T(8,128)(2,1)} %embed_ref.1) | copy-start | bytes 645124
  3.6 0.9 %copy-start.3 = (bf16[768,140]{0,1:T(8,128)(2,1)S(1)}, bf16[768,140]{0,1:T(8,128)(2,1)}, u32[]{:S(2)}) copy-start(bf16[768,140]{0,1:T(8,128)(2,1)} %param.16) | copy-start | bytes 645124
  4.6 0.9 %copy-start.4 = (bf16[768,96]{0,1:T(8,128)(2,1)S(1)}, bf16[768,96]{0,1:T(8,128)(2,1)}, u32[]{:S(2)}) copy-start(bf16[768,96]{0,1:T(8,128)(2,1)} %param.15) | copy-start | bytes 442372
  5.5 0.7 copy-start.9
  6.2 0.7 copy-start.10

commit v3 on v2

--- a/solution.py
+++ b/solution.py
@@ -271,10 +271,21 @@
 
 def forecast_and_analyse(
     heads,
+    x_hbm,
+    embed_hbm,
+    qkv_hbm,
+    comb_hbm,
+    dec_hbm,
+    scale_hbm,
+    load_hbm,
+    grid_hbm,
+    dom_hbm,
+    chan_hbm,
+    read_hbm,
+    noise_hbm,
+    out_ref,
     x_ref,
     embed_ref,
-    qkv_ref,
-    comb_ref,
     dec_ref,
     scale_ref,
     load_ref,
@@ -283,7 +294,6 @@
     chan_ref,
     read_ref,
     noise_ref,
-    out_ref,
     g_embed,
     g_qkv,
     g_comb,
@@ -304,6 +314,7 @@
     t_recv,
     a_send,
     a_recv,
+    l_sem,
 ):
     bf16, f32 = jnp.bfloat16, jnp.float32
     me = lax.axis_index("mem")
@@ -332,6 +343,32 @@
     count = grid_ref.shape[2]
     variables = load_ref.shape[1]
 
+    def own_rows(held):
+        rows = held.shape[0] // n
+        return held.at[pl.ds(pl.multiple_of(me * rows, 16), rows)]
+
+    local = [
+        pltpu.make_async_copy(source, target, l_sem.at[i])
+        for i, (source, target) in enumerate(
+            (
+                (embed_hbm, embed_ref),
+                (qkv_hbm, own_rows(g_qkv)),
+                (x_hbm, x_ref),
+                (comb_hbm, own_rows(g_comb)),
+                (dec_hbm, dec_ref),
+                (load_hbm, load_ref),
+                (grid_hbm, grid_ref),
+                (chan_hbm, chan_ref),
+                (dom_hbm, dom_ref),
+                (read_hbm, read_ref),
+                (noise_hbm, noise_ref),
+                (scale_hbm, scale_ref),
+            )
+        )
+    ]
+    for fetched in local:
+        fetched.start()
+
     barrier = pltpu.get_barrier_semaphore()
     for step in range(1, n):
         pl.semaphore_signal(
@@ -425,6 +462,34 @@
         for kind, owner in ((12, x_nb), (13, y_nb), (14, diag)):
             arrived(w, kind, owner + to_sib, 2 * (1 - odd) * t, t)
 
+    def own_whole(w):
+        rows = gathered[w].shape[0] // n
+        send(w, 1, me, 0, rows, "x")
+        send(w, 2, me, 0, rows, "y")
+        send(w, 0, me, 0, rows, "sib")
+
+    def pass_whole(w):
+        rows = gathered[w].shape[0] // n
+        upper = rows // 32 * 16
+        arrived(w, 1, x_nb, 0, rows)
+        send(w, 5, x_nb, 0, upper, "y")
+        send(w, 3, x_nb, 0, rows, "sib")
+        arrived(w, 2, y_nb, 0, rows)
+        send(w, 6, y_nb, upper, rows - upper, "x")
+        send(w, 4, y_nb, 0, rows, "sib")
+
+    def pass_corner(w):
+        rows = gathered[w].shape[0] // n
+        upper = rows // 32 * 16
+        arrived(w, 5, diag, 0, upper)
+        arrived(w, 6, diag, upper, rows - upper)
+        send(w, 7, diag, 0, rows, "sib")
+
+    def complete_whole(w):
+        rows = gathered[w].shape[0] // n
+        for kind, owner in ((0, me), (3, x_nb), (4, y_nb), (7, diag)):
+            arrived(w, kind, owner + to_sib, 0, rows)
+
     def keep_own(w, ref):
         block = gathered[w].shape[0] // n
         rows = ref.shape[0] // 16 * 16
@@ -438,13 +503,15 @@
 
     EMBED, QKV, COMB, DEC = 0, 1, 2, 3
 
+    local[0].wait()
     keep_own(EMBED, embed_ref)
-    keep_own(QKV, qkv_ref)
     pl.semaphore_wait(barrier, n + 1)
     own_first(EMBED)
     own_second(EMBED)
+    local[1].wait()
     own_first(QKV)
-    keep_own(COMB, comb_ref)
+    for fetched in local[2:]:
+        fetched.wait()
     keep_own(DEC, dec_ref)
 
     row = iota((tokens, tokens), 0)
@@ -481,10 +548,9 @@
     ).astype(bf16)
 
     pass_diagonal(EMBED)
-    own_first(COMB)
     pass_first(QKV)
     pass_partner(EMBED)
-    own_second(COMB)
+    own_whole(COMB)
     complete(EMBED)
 
     hidden = dot(x_pad[...], g_embed[...]).astype(bf16)
@@ -507,19 +573,13 @@
     sends.append(westward)
 
     pass_second(QKV)
-    own_first(DEC)
-    pass_first(COMB)
     pass_diagonal(QKV)
-    own_second(DEC)
-    pass_second(COMB)
+    own_whole(DEC)
     pass_partner(QKV)
     complete(QKV)
-    qkv_buf[half:, :] = dot_nt(window[half:, :], g_qkv[...]).astype(bf16)
-    pass_first(DEC)
-    pass_diagonal(COMB)
     westward.wait_recv()
-    qkv_buf[:half, :] = dot_nt(window[:half, :], g_qkv[...]).astype(bf16)
-    pass_second(DEC)
+    qkv_buf[...] = dot_nt(window[...], g_qkv[...]).astype(bf16)
+    pass_whole(COMB)
 
     side = span // heads
     pair = 2 * side
@@ -543,7 +603,11 @@
             start = pair * p
             query = unit_pair(rows, start)
             key = keys[p]
-            scales = jnp.where(key_of < tokens, scale_ref[2 * p], scale_ref[2 * p + 1])
+            scales = jnp.where(
+                key_of < tokens,
+                scale_ref[:, 2 * p : 2 * p + 1],
+                scale_ref[:, 2 * p + 1 : 2 * p + 2],
+            )
             weights = jnp.where(same_member, jnp.exp(dot_nt(query, key) * scales), 0.0).astype(bf16)
             value = qkv_buf[:, 2 * span + start : 2 * span + start + pair]
             value = jnp.concatenate([value * first, value * second], axis=0)
@@ -558,16 +622,14 @@
     eastward = along_tile(1, ctx.at[pl.ds(0, half)], from_west, east)
     eastward.start()
     sends.append(eastward)
-    pass_partner(COMB)
-    pass_diagonal(DEC)
+    pass_corner(COMB)
+    pass_whole(DEC)
     attend(slice(half, tokens), range(heads // 2))
-    complete(COMB)
-    pass_partner(DEC)
-    own_half = dot_nt(ctx[half:, :], g_comb[...])
+    complete_whole(COMB)
+    pass_corner(DEC)
     eastward.wait_recv()
-    mixed = hidden.astype(f32) + jnp.concatenate(
-        [dot_nt(from_west[...], g_comb[...]), own_half], axis=0
-    )
+    context = jnp.concatenate([from_west[...], ctx[half:, :]], axis=0)
+    mixed = hidden.astype(f32) + dot_nt(context, g_comb[...])
     latent = layer_norm(mixed).astype(bf16)
     by_region = picked(
         tokens,
@@ -607,7 +669,7 @@
             ).wait_recv()
 
     exchange(0, lat_send, lat_recv)
-    complete(DEC)
+    complete_whole(DEC)
     exchanged(0, lat_send, lat_recv)
 
     regions = n
@@ -685,7 +747,7 @@
     span = patch_lifting.shape[1]
     padded = -(-patch_lifting.shape[0] // 48) * 48
     vmem = pl.BlockSpec(memory_space=pltpu.VMEM)
-    smem = pl.BlockSpec(memory_space=pltpu.SMEM)
+    hbm = pl.BlockSpec(memory_space=pltpu.HBM)
 
     def held(*shape):
         return pltpu.VMEM(shape, jnp.bfloat16)
@@ -693,9 +755,15 @@
     out = pl.pallas_call(
         functools.partial(forecast_and_analyse, cosine_logit_scale.shape[0]),
         out_shape=jax.ShapeDtypeStruct((tokens, feats), jnp.bfloat16),
-        in_specs=[vmem] * 5 + [smem] + [vmem] * 6,
+        in_specs=[hbm] * 12,
         out_specs=vmem,
         scratch_shapes=[
+            held(tokens, feats),
+            held(*patch_lifting.shape),
+            held(decoder_linear_map.shape[1], span),
+            pltpu.VMEM((1, cosine_logit_scale.shape[0]), jnp.float32),
+            held(*sensor_variable_loadings.shape),
+            *[pltpu.VMEM(sensor.shape, sensor.dtype) for sensor in sensors],
             held(padded * n, span),
             held(query_keyvalue_lift.shape[1] * n, span),
             held(output_combiner.shape[1] * n, span),
@@ -716,9 +784,10 @@
             pltpu.SemaphoreType.DMA((2,)),
             pltpu.SemaphoreType.DMA((2 * n,)),
             pltpu.SemaphoreType.DMA((2 * n,)),
+            pltpu.SemaphoreType.DMA((12,)),
         ],
         compiler_params=pltpu.CompilerParams(
-            collective_id=0, has_side_effects=True, vmem_limit_bytes=48 * 1024 * 1024
+            collective_id=0, has_side_effects=True, vmem_limit_bytes=63 * 1024 * 1024
         ),
         cost_estimate=pl.CostEstimate(
             flops=2 * tokens * span * (3 * feats + 4 * span),
@@ -731,7 +800,7 @@
         query_keyvalue_lift.T,
         output_combiner.T,
         decoder_linear_map.T,
-        cosine_logit_scale,
+        cosine_logit_scale.reshape(1, -1),
         sensor_variable_loadings,
         *sensors,
     )

time: 68.9 us -> 56.8 us (0.82)
  Pallas kernels: 61 us -> 54.9 us
  local copies, waits for them, and re-layouts: 7.55 us -> 1.7 us
    pallas_call x1, Pallas kernels: 61 us -> 54.9 us  [per_device_fused(): pl.pallas_call(functools.partial(forecast_and_analyse, cosine_logit_scale...]
    unnamed x25 -> x1, local copies, waits for them, and re-layouts: 7.55 us -> 1.7 us
where the time goes in v3:
time: 56.8 us; the launch traced here: 56.7 us
  Pallas kernels  54.9 us (97%)
  local copies, waits for them, and re-layouts  1.7 us (3%)
    pallas_call x1, Pallas kernels, per_device_fused(): pl.pallas_call(functools.partial(forecast_and_analyse, cosine_logit_scale...  54.9 us
    unnamed x1, local copies, waits for them, and re-layouts  1.7 us

profile of v3, /device:TPU:0, one launch (start us, length us, event | category | flops | bytes accessed | tf_op | source)
XLA Modules:
  0.0 56.7 jit_solution(11820704075539444593)
XLA Ops:
  0.0 54.9 %shard_map.118 = bf16[128,1120]{1,0:T(8,128)(2,1)} custom-call(bf16[128,1120]{1,0:T(8,128)(2,1)} %bitcast.8, bf16[140,768]{1,0:T(8,128)(2,1)} %embed_hbm.1, bf16[288,768]{1,0:T(8,128)(2,1)} %bitcast.7, bf16[96,768]{1,0:T(8,128)(2,1)} %bitcast.10, bf16[140,768]{1,0:T(8,128)(2,1)} %bitcast.9, f32[1,12]{1,0:T(1,128)} %bitcast.11, bf16[16,70]{1,0:T(8,128)(2,1)} %load_hbm.1, ...), custom_call_target="tpu_custom_call" | custom-call | flops 1264582656 | bytes 16777216 | tf_op jit(solution)/shard_map/pallas_call | solution.py:755
  55.0 1.7 %copy.14 = bf16[2,8,8,1120]{3,2,1,0:T(8,128)(2,1)} copy(bf16[2,8,8,1120]{3,2,1,0:T(8,128)(2,1)} %bitcast.6) | data formatting | bytes 573440

commit v4 on v3

--- a/solution.py
+++ b/solution.py
@@ -508,11 +508,8 @@
     pl.semaphore_wait(barrier, n + 1)
     own_first(EMBED)
     own_second(EMBED)
-    local[1].wait()
-    own_first(QKV)
-    for fetched in local[2:]:
+    for fetched in local[1:]:
         fetched.wait()
-    keep_own(DEC, dec_ref)
 
     row = iota((tokens, tokens), 0)
     by_half = picked(
@@ -526,8 +523,36 @@
 
     pass_first(EMBED)
     pass_second(EMBED)
+    own_first(QKV)
     own_second(QKV)
-
+    pass_diagonal(EMBED)
+    pass_partner(EMBED)
+    complete(EMBED)
+    pass_first(QKV)
+
+    hidden = dot(x_pad[...], g_embed[...]).astype(bf16)
+    normed = layer_norm(hidden).astype(bf16)
+    to_west[...] = normed[:half]
+    window[half:, :] = normed[half:]
+
+    def along_tile(index, source, target, way):
+        return pltpu.make_async_remote_copy(
+            src_ref=source,
+            dst_ref=target,
+            send_sem=t_send.at[index],
+            recv_sem=t_recv.at[index],
+            device_id=(me, way),
+            device_id_type=MESH,
+        )
+
+    westward = along_tile(0, to_west, window.at[pl.ds(0, half)], west)
+    westward.start()
+    sends.append(westward)
+
+    pass_second(QKV)
+    own_whole(COMB)
+
+    keep_own(DEC, dec_ref)
     within = iota((n, padded, variables), 1)
     within = within - jnp.where(within >= variables, variables, 0)
     pick_variable = one_hot(within == iota((n, padded, variables), 2)).reshape(width, variables)
@@ -547,39 +572,14 @@
         slot.reshape(width, count) == jnp.broadcast_to(point_row, (width, count)), mapping, 0.0
     ).astype(bf16)
 
-    pass_diagonal(EMBED)
-    pass_first(QKV)
-    pass_partner(EMBED)
-    own_whole(COMB)
-    complete(EMBED)
-
-    hidden = dot(x_pad[...], g_embed[...]).astype(bf16)
-    normed = layer_norm(hidden).astype(bf16)
-    to_west[...] = normed[:half]
-    window[half:, :] = normed[half:]
-
-    def along_tile(index, source, target, way):
-        return pltpu.make_async_remote_copy(
-            src_ref=source,
-            dst_ref=target,
-            send_sem=t_send.at[index],
-            recv_sem=t_recv.at[index],
-            device_id=(me, way),
-            device_id_type=MESH,
-        )
-
-    westward = along_tile(0, to_west, window.at[pl.ds(0, half)], west)
-    westward.start()
-    sends.append(westward)
-
-    pass_second(QKV)
     pass_diagonal(QKV)
+    pass_whole(COMB)
     own_whole(DEC)
     pass_partner(QKV)
     complete(QKV)
     westward.wait_recv()
     qkv_buf[...] = dot_nt(window[...], g_qkv[...]).astype(bf16)
-    pass_whole(COMB)
+    pass_corner(COMB)
 
     side = span // heads
     pair = 2 * side
@@ -622,7 +622,6 @@
     eastward = along_tile(1, ctx.at[pl.ds(0, half)], from_west, east)
     eastward.start()
     sends.append(eastward)
-    pass_corner(COMB)
     pass_whole(DEC)
     attend(slice(half, tokens), range(heads // 2))
     complete_whole(COMB)
@@ -720,6 +719,8 @@
     )
     pos_send[...] = posterior.astype(bf16)
     exchange(1, pos_send, pos_recv)
+    for sent in sends[: 1 - n]:
+        sent.wait_send()
     exchanged(1, pos_send, pos_recv)
     by_member = picked(tokens, ((row >> 3) & 7) * 16 + (row >> 6) * 8 + (row & 7))
     analysed = dot_nt(dot(by_member, pos_recv[...]).astype(bf16), g_dec[...])
@@ -727,7 +728,7 @@
         out_ref[:, piece * d : piece * (d + 1)] = analysed[
             :, padded * d : padded * d + piece
         ].astype(bf16)
-    for sent in sends:
+    for sent in sends[1 - n :]:
         sent.wait_send()
 
 

time: 56.8 us -> 57.8 us (1.018)
  Pallas kernels: 54.9 us -> 56 us
    pallas_call x1, Pallas kernels: 54.9 us -> 56 us  [per_device_fused(): pl.pallas_call(functools.partial(forecast_and_analyse, cosine_logit_scale...]
where the time goes in v4:
time: 57.8 us; the launch traced here: 57.7 us
  Pallas kernels  56 us (97%)
  local copies, waits for them, and re-layouts  1.7 us (3%)
    pallas_call x1, Pallas kernels, per_device_fused(): pl.pallas_call(functools.partial(forecast_and_analyse, cosine_logit_scale...  56 us
    unnamed x1, local copies, waits for them, and re-layouts  1.7 us

profile of v4, /device:TPU:0, one launch (start us, length us, event | category | flops | bytes accessed | tf_op | source)
XLA Modules:
  0.0 57.7 jit_solution(16847959294095498100)
XLA Ops:
  0.0 56.0 %shard_map.118 = bf16[128,1120]{1,0:T(8,128)(2,1)} custom-call(bf16[128,1120]{1,0:T(8,128)(2,1)} %bitcast.8, bf16[140,768]{1,0:T(8,128)(2,1)} %embed_hbm.1, bf16[288,768]{1,0:T(8,128)(2,1)} %bitcast.7, bf16[96,768]{1,0:T(8,128)(2,1)} %bitcast.10, bf16[140,768]{1,0:T(8,128)(2,1)} %bitcast.9, f32[1,12]{1,0:T(1,128)} %bitcast.11, bf16[16,70]{1,0:T(8,128)(2,1)} %load_hbm.1, ...), custom_call_target="tpu_custom_call" | custom-call | flops 1264582656 | bytes 16777216 | tf_op jit(solution)/shard_map/pallas_call | solution.py:756
  56.0 1.7 %copy.14 = bf16[2,8,8,1120]{3,2,1,0:T(8,128)(2,1)} copy(bf16[2,8,8,1120]{3,2,1,0:T(8,128)(2,1)} %bitcast.6) | data formatting | bytes 573440

commit v5 on v3

--- a/solution.py
+++ b/solution.py
@@ -247,10 +247,22 @@
 def fine(left, right):
     left_high, left_low = two_terms(left)
     right_high, right_low = two_terms(right)
-    return dot(
-        jnp.concatenate([left_high, left_low], axis=1),
-        jnp.concatenate([right_high, right_high], axis=0),
-    ) + dot(left_high, right_low)
+    left_terms = jnp.concatenate([left_high, left_low], axis=1)
+    if right.shape[1] > 128:
+        return dot(left_terms, jnp.concatenate([right_high, right_high], axis=0)) + dot(
+            left_high, right_low
+        )
+    both = dot(
+        left_terms,
+        jnp.concatenate(
+            [
+                jnp.concatenate([right_high, right_low], axis=1),
+                jnp.concatenate([right_high, jnp.zeros_like(right_low)], axis=1),
+            ],
+            axis=0,
+        ),
+    )
+    return both[:, : right.shape[1]] + both[:, right.shape[1] :]
 
 
 def fine_nt(left, right):
@@ -508,11 +520,8 @@
     pl.semaphore_wait(barrier, n + 1)
     own_first(EMBED)
     own_second(EMBED)
-    local[1].wait()
-    own_first(QKV)
-    for fetched in local[2:]:
+    for fetched in local[1:]:
         fetched.wait()
-    keep_own(DEC, dec_ref)
 
     row = iota((tokens, tokens), 0)
     by_half = picked(
@@ -526,8 +535,9 @@
 
     pass_first(EMBED)
     pass_second(EMBED)
+    own_first(QKV)
     own_second(QKV)
-
+    keep_own(DEC, dec_ref)
     within = iota((n, padded, variables), 1)
     within = within - jnp.where(within >= variables, variables, 0)
     pick_variable = one_hot(within == iota((n, padded, variables), 2)).reshape(width, variables)
@@ -548,10 +558,9 @@
     ).astype(bf16)
 
     pass_diagonal(EMBED)
+    pass_partner(EMBED)
+    complete(EMBED)
     pass_first(QKV)
-    pass_partner(EMBED)
-    own_whole(COMB)
-    complete(EMBED)
 
     hidden = dot(x_pad[...], g_embed[...]).astype(bf16)
     normed = layer_norm(hidden).astype(bf16)
@@ -573,13 +582,16 @@
     sends.append(westward)
 
     pass_second(QKV)
+    own_whole(COMB)
+
     pass_diagonal(QKV)
+    pass_whole(COMB)
     own_whole(DEC)
     pass_partner(QKV)
     complete(QKV)
     westward.wait_recv()
     qkv_buf[...] = dot_nt(window[...], g_qkv[...]).astype(bf16)
-    pass_whole(COMB)
+    pass_corner(COMB)
 
     side = span // heads
     pair = 2 * side
@@ -622,19 +634,18 @@
     eastward = along_tile(1, ctx.at[pl.ds(0, half)], from_west, east)
     eastward.start()
     sends.append(eastward)
-    pass_corner(COMB)
     pass_whole(DEC)
     attend(slice(half, tokens), range(heads // 2))
     complete_whole(COMB)
     pass_corner(DEC)
+    by_region = picked(
+        tokens,
+        ((row >> 2) & 1) * 64 + ((row >> 3) & 1) * 32 + (row >> 4) * 4 + (row & 3),
+    )
     eastward.wait_recv()
     context = jnp.concatenate([from_west[...], ctx[half:, :]], axis=0)
     mixed = hidden.astype(f32) + dot_nt(context, g_comb[...])
     latent = layer_norm(mixed).astype(bf16)
-    by_region = picked(
-        tokens,
-        ((row >> 2) & 1) * 64 + ((row >> 3) & 1) * 32 + (row >> 4) * 4 + (row & 3),
-    )
     lat_send[...] = dot(by_region, latent).astype(bf16)
 
     block = tokens // n
@@ -670,27 +681,32 @@
 
     exchange(0, lat_send, lat_recv)
     complete_whole(DEC)
-    exchanged(0, lat_send, lat_recv)
-
     regions = n
     members = tokens // regions
+    region3 = iota((members, regions, count), 1)
+    on_token = jnp.where(region3 == token_row[None], 1.0, 0.0)
+    in_region = jnp.where(region3 == dom_row[None], 1.0, 0.0).reshape(tokens, count)
+    distance = (token_row - dom_row).astype(f32)
+    noise = noise_ref[0]
+    obs_weight = jnp.exp(-0.5 * distance * distance) / (noise * noise)
+    in_region_weight = in_region * obs_weight
+    reading = read_ref[0]
+    unit = jnp.where(row == iota((tokens, tokens), 1), 1.0, 0.0)
+    same_region = (row & (regions - 1)) == (iota((tokens, tokens), 1) & (regions - 1))
+    by_member = picked(tokens, ((row >> 3) & 7) * 16 + (row >> 6) * 8 + (row & 7))
+    exchanged(0, lat_send, lat_recv)
+
     values = lat_recv[...]
     prior = dot_nt(values, g_dec[...]).astype(bf16)
     samples = dot(prior, mapping).reshape(members, regions, count)
-    region3 = iota((members, regions, count), 1)
-    samples = jnp.where(region3 == token_row[None], samples, 0.0)
-    ens_obs = jnp.sum(samples, axis=1, keepdims=True)
+    ens_obs = jnp.sum(samples * on_token, axis=1, keepdims=True)
     mean_obs = jnp.mean(ens_obs, axis=0, keepdims=True)
-    in_region = region3 == dom_row[None]
-    pert = jnp.where(in_region, ens_obs - mean_obs, 0.0).reshape(tokens, count)
-    innovation = read_ref[0] - mean_obs[0]
-    distance = (token_row - dom_row).astype(f32)
-    noise = noise_ref[0]
-    obs_weight = jnp.exp(-0.5 * distance * distance) / (noise * noise)
-    weighted = pert * obs_weight
+    pert = jnp.broadcast_to(ens_obs - mean_obs, samples.shape).reshape(tokens, count)
+    innovation = reading - mean_obs[0]
+    weighted = pert * in_region_weight
+    pert = pert * in_region
     gram = fine_nt(weighted, pert)
     drive = fine_nt(jnp.broadcast_to(innovation, (tokens, count)), weighted)
-    unit = jnp.where(row == iota((tokens, tokens), 1), 1.0, 0.0)
     system = unit + gram * (1.0 / (members - 1.0))
     sums = jnp.sum(jnp.abs(system), axis=1, keepdims=True).reshape(members, regions, 1)
     bound = jnp.broadcast_to(
@@ -710,7 +726,6 @@
     root = inverse_root * lax.rsqrt(bound)
     inner = fine(drive, root)
     mean_weight = fine(inner, root) * (1.0 / (members - 1.0))
-    same_region = (row & (regions - 1)) == (iota((tokens, tokens), 1) & (regions - 1))
     transform_back = jnp.where(same_region, root + mean_weight, 0.0)
     latents = values.astype(f32).reshape(members, regions, span)
     center = jnp.mean(latents, axis=0, keepdims=True)
@@ -720,14 +735,15 @@
     )
     pos_send[...] = posterior.astype(bf16)
     exchange(1, pos_send, pos_recv)
+    for sent in sends[: 1 - n]:
+        sent.wait_send()
     exchanged(1, pos_send, pos_recv)
-    by_member = picked(tokens, ((row >> 3) & 7) * 16 + (row >> 6) * 8 + (row & 7))
     analysed = dot_nt(dot(by_member, pos_recv[...]).astype(bf16), g_dec[...])
     for d in range(n):
         out_ref[:, piece * d : piece * (d + 1)] = analysed[
             :, padded * d : padded * d + piece
         ].astype(bf16)
-    for sent in sends:
+    for sent in sends[1 - n :]:
         sent.wait_send()
 
 

time: 56.8 us -> 57.7 us (1.016)
  Pallas kernels: 54.9 us -> 55.8 us
    pallas_call x1, Pallas kernels: 54.9 us -> 55.8 us  [per_device_fused(): pl.pallas_call(functools.partial(forecast_and_analyse, cosine_logit_scale...]
where the time goes in v5:
time: 57.7 us; the launch traced here: 57.5 us
  Pallas kernels  55.8 us (97%)
  local copies, waits for them, and re-layouts  1.7 us (3%)
    pallas_call x1, Pallas kernels, per_device_fused(): pl.pallas_call(functools.partial(forecast_and_analyse, cosine_logit_scale...  55.8 us
    unnamed x1, local copies, waits for them, and re-layouts  1.7 us

profile of v5, /device:TPU:0, one launch (start us, length us, event | category | flops | bytes accessed | tf_op | source)
XLA Modules:
  0.0 57.5 jit_solution(15464585522006477494)
XLA Ops:
  0.0 55.8 %shard_map.118 = bf16[128,1120]{1,0:T(8,128)(2,1)} custom-call(bf16[128,1120]{1,0:T(8,128)(2,1)} %bitcast.8, bf16[140,768]{1,0:T(8,128)(2,1)} %embed_hbm.1, bf16[288,768]{1,0:T(8,128)(2,1)} %bitcast.7, bf16[96,768]{1,0:T(8,128)(2,1)} %bitcast.10, bf16[140,768]{1,0:T(8,128)(2,1)} %bitcast.9, f32[1,12]{1,0:T(1,128)} %bitcast.11, bf16[16,70]{1,0:T(8,128)(2,1)} %load_hbm.1, ...), custom_call_target="tpu_custom_call" | custom-call | flops 1264582656 | bytes 16777216 | tf_op jit(solution)/shard_map/pallas_call | solution.py:771
  55.8 1.7 %copy.14 = bf16[2,8,8,1120]{3,2,1,0:T(8,128)(2,1)} copy(bf16[2,8,8,1120]{3,2,1,0:T(8,128)(2,1)} %bitcast.6) | data formatting | bytes 573440

commit v6 on v5

--- a/solution.py
+++ b/solution.py
@@ -518,9 +518,10 @@
     local[0].wait()
     keep_own(EMBED, embed_ref)
     pl.semaphore_wait(barrier, n + 1)
-    own_first(EMBED)
-    own_second(EMBED)
-    for fetched in local[1:]:
+    own_whole(EMBED)
+    local[1].wait()
+    own_first(QKV)
+    for fetched in local[2:]:
         fetched.wait()
 
     row = iota((tokens, tokens), 0)
@@ -533,9 +534,7 @@
     for d in range(n):
         x_pad[:, padded * d : padded * d + piece] = x_rows[:, piece * d : piece * (d + 1)]
 
-    pass_first(EMBED)
-    pass_second(EMBED)
-    own_first(QKV)
+    pass_whole(EMBED)
     own_second(QKV)
     keep_own(DEC, dec_ref)
     within = iota((n, padded, variables), 1)
@@ -557,10 +556,10 @@
         slot.reshape(width, count) == jnp.broadcast_to(point_row, (width, count)), mapping, 0.0
     ).astype(bf16)
 
-    pass_diagonal(EMBED)
-    pass_partner(EMBED)
-    complete(EMBED)
+    pass_corner(EMBED)
     pass_first(QKV)
+    own_whole(COMB)
+    complete_whole(EMBED)
 
     hidden = dot(x_pad[...], g_embed[...]).astype(bf16)
     normed = layer_norm(hidden).astype(bf16)
@@ -582,16 +581,14 @@
     sends.append(westward)
 
     pass_second(QKV)
-    own_whole(COMB)
 
     pass_diagonal(QKV)
-    pass_whole(COMB)
     own_whole(DEC)
     pass_partner(QKV)
     complete(QKV)
     westward.wait_recv()
     qkv_buf[...] = dot_nt(window[...], g_qkv[...]).astype(bf16)
-    pass_corner(COMB)
+    pass_whole(COMB)
 
     side = span // heads
     pair = 2 * side
@@ -634,6 +631,7 @@
     eastward = along_tile(1, ctx.at[pl.ds(0, half)], from_west, east)
     eastward.start()
     sends.append(eastward)
+    pass_corner(COMB)
     pass_whole(DEC)
     attend(slice(half, tokens), range(heads // 2))
     complete_whole(COMB)

time: 57.7 us -> 57.2 us (level)
  no operation moved by 1% of the time
where the time goes in v6:
time: 57.2 us; the launch traced here: 57 us
  Pallas kernels  55.3 us (97%)
  local copies, waits for them, and re-layouts  1.7 us (3%)
    pallas_call x1, Pallas kernels, per_device_fused(): pl.pallas_call(functools.partial(forecast_and_analyse, cosine_logit_scale...  55.3 us
    unnamed x1, local copies, waits for them, and re-layouts  1.7 us

profile of v6, /device:TPU:0, one launch (start us, length us, event | category | flops | bytes accessed | tf_op | source)
XLA Modules:
  0.0 57.0 jit_solution(12746552054887226754)
XLA Ops:
  0.0 55.3 %shard_map.118 = bf16[128,1120]{1,0:T(8,128)(2,1)} custom-call(bf16[128,1120]{1,0:T(8,128)(2,1)} %bitcast.8, bf16[140,768]{1,0:T(8,128)(2,1)} %embed_hbm.1, bf16[288,768]{1,0:T(8,128)(2,1)} %bitcast.7, bf16[96,768]{1,0:T(8,128)(2,1)} %bitcast.10, bf16[140,768]{1,0:T(8,128)(2,1)} %bitcast.9, f32[1,12]{1,0:T(1,128)} %bitcast.11, bf16[16,70]{1,0:T(8,128)(2,1)} %load_hbm.1, ...), custom_call_target="tpu_custom_call" | custom-call | flops 1264582656 | bytes 16777216 | tf_op jit(solution)/shard_map/pallas_call | solution.py:769
  55.3 1.7 %copy.14 = bf16[2,8,8,1120]{3,2,1,0:T(8,128)(2,1)} copy(bf16[2,8,8,1120]{3,2,1,0:T(8,128)(2,1)} %bitcast.6) | data formatting | bytes 573440

commit v7 on v6

--- a/solution.py
+++ b/solution.py
@@ -583,12 +583,13 @@
     pass_second(QKV)
 
     pass_diagonal(QKV)
+    pass_whole(COMB)
     own_whole(DEC)
     pass_partner(QKV)
     complete(QKV)
     westward.wait_recv()
     qkv_buf[...] = dot_nt(window[...], g_qkv[...]).astype(bf16)
-    pass_whole(COMB)
+    pass_corner(COMB)
 
     side = span // heads
     pair = 2 * side
@@ -631,11 +632,9 @@
     eastward = along_tile(1, ctx.at[pl.ds(0, half)], from_west, east)
     eastward.start()
     sends.append(eastward)
-    pass_corner(COMB)
+    attend(slice(half, tokens), range(heads // 2))
     pass_whole(DEC)
-    attend(slice(half, tokens), range(heads // 2))
     complete_whole(COMB)
-    pass_corner(DEC)
     by_region = picked(
         tokens,
         ((row >> 2) & 1) * 64 + ((row >> 3) & 1) * 32 + (row >> 4) * 4 + (row & 3),
@@ -678,7 +677,7 @@
             ).wait_recv()
 
     exchange(0, lat_send, lat_recv)
-    complete_whole(DEC)
+    pass_corner(DEC)
     regions = n
     members = tokens // regions
     region3 = iota((members, regions, count), 1)
@@ -692,6 +691,7 @@
     unit = jnp.where(row == iota((tokens, tokens), 1), 1.0, 0.0)
     same_region = (row & (regions - 1)) == (iota((tokens, tokens), 1) & (regions - 1))
     by_member = picked(tokens, ((row >> 3) & 7) * 16 + (row >> 6) * 8 + (row & 7))
+    complete_whole(DEC)
     exchanged(0, lat_send, lat_recv)
 
     values = lat_recv[...]

time: 57.2 us -> 55.5 us (0.970)
  Pallas kernels: 55.3 us -> 53.7 us
    pallas_call x1, Pallas kernels: 55.3 us -> 53.7 us  [per_device_fused(): pl.pallas_call(functools.partial(forecast_and_analyse, cosine_logit_scale...]
where the time goes in v7:
time: 55.5 us; the launch traced here: 55.4 us
  Pallas kernels  53.7 us (97%)
  local copies, waits for them, and re-layouts  1.7 us (3%)
    pallas_call x1, Pallas kernels, per_device_fused(): pl.pallas_call(functools.partial(forecast_and_analyse, cosine_logit_scale...  53.7 us
    unnamed x1, local copies, waits for them, and re-layouts  1.7 us

profile of v7, /device:TPU:0, one launch (start us, length us, event | category | flops | bytes accessed | tf_op | source)
XLA Modules:
  0.0 55.4 jit_solution(2713803734116407889)
XLA Ops:
  0.0 53.7 %shard_map.118 = bf16[128,1120]{1,0:T(8,128)(2,1)} custom-call(bf16[128,1120]{1,0:T(8,128)(2,1)} %bitcast.8, bf16[140,768]{1,0:T(8,128)(2,1)} %embed_hbm.1, bf16[288,768]{1,0:T(8,128)(2,1)} %bitcast.7, bf16[96,768]{1,0:T(8,128)(2,1)} %bitcast.10, bf16[140,768]{1,0:T(8,128)(2,1)} %bitcast.9, f32[1,12]{1,0:T(1,128)} %bitcast.11, bf16[16,70]{1,0:T(8,128)(2,1)} %load_hbm.1, ...), custom_call_target="tpu_custom_call" | custom-call | flops 1264582656 | bytes 16777216 | tf_op jit(solution)/shard_map/pallas_call | solution.py:769
  53.7 1.7 %copy.14 = bf16[2,8,8,1120]{3,2,1,0:T(8,128)(2,1)} copy(bf16[2,8,8,1120]{3,2,1,0:T(8,128)(2,1)} %bitcast.6) | data formatting | bytes 573440

commit v8 on v7

--- a/solution.py
+++ b/solution.py
@@ -518,7 +518,8 @@
     local[0].wait()
     keep_own(EMBED, embed_ref)
     pl.semaphore_wait(barrier, n + 1)
-    own_whole(EMBED)
+    own_first(EMBED)
+    own_second(EMBED)
     local[1].wait()
     own_first(QKV)
     for fetched in local[2:]:
@@ -534,7 +535,8 @@
     for d in range(n):
         x_pad[:, padded * d : padded * d + piece] = x_rows[:, piece * d : piece * (d + 1)]
 
-    pass_whole(EMBED)
+    pass_first(EMBED)
+    pass_second(EMBED)
     own_second(QKV)
     keep_own(DEC, dec_ref)
     within = iota((n, padded, variables), 1)
@@ -556,10 +558,11 @@
         slot.reshape(width, count) == jnp.broadcast_to(point_row, (width, count)), mapping, 0.0
     ).astype(bf16)
 
-    pass_corner(EMBED)
+    pass_diagonal(EMBED)
     pass_first(QKV)
+    pass_partner(EMBED)
     own_whole(COMB)
-    complete_whole(EMBED)
+    complete(EMBED)
 
     hidden = dot(x_pad[...], g_embed[...]).astype(bf16)
     normed = layer_norm(hidden).astype(bf16)

time: 55.5 us -> 55.9 us (level)
  no operation moved by 1% of the time
where the time goes in v8:
time: 55.9 us; the launch traced here: 55.7 us
  Pallas kernels  54 us (97%)
  local copies, waits for them, and re-layouts  1.7 us (3%)
    pallas_call x1, Pallas kernels, per_device_fused(): pl.pallas_call(functools.partial(forecast_and_analyse, cosine_logit_scale...  54 us
    unnamed x1, local copies, waits for them, and re-layouts  1.7 us

profile of v8, /device:TPU:0, one launch (start us, length us, event | category | flops | bytes accessed | tf_op | source)
XLA Modules:
  0.0 55.7 jit_solution(5394404358866349334)
XLA Ops:
  0.0 54.0 %shard_map.118 = bf16[128,1120]{1,0:T(8,128)(2,1)} custom-call(bf16[128,1120]{1,0:T(8,128)(2,1)} %bitcast.8, bf16[140,768]{1,0:T(8,128)(2,1)} %embed_hbm.1, bf16[288,768]{1,0:T(8,128)(2,1)} %bitcast.7, bf16[96,768]{1,0:T(8,128)(2,1)} %bitcast.10, bf16[140,768]{1,0:T(8,128)(2,1)} %bitcast.9, f32[1,12]{1,0:T(1,128)} %bitcast.11, bf16[16,70]{1,0:T(8,128)(2,1)} %load_hbm.1, ...), custom_call_target="tpu_custom_call" | custom-call | flops 1264582656 | bytes 16777216 | tf_op jit(solution)/shard_map/pallas_call | solution.py:772
  54.0 1.7 %copy.14 = bf16[2,8,8,1120]{3,2,1,0:T(8,128)(2,1)} copy(bf16[2,8,8,1120]{3,2,1,0:T(8,128)(2,1)} %bitcast.6) | data formatting | bytes 573440
